TPU v7x, 512 devices: a whole 4x4x16 slice. The times are simulated.
512 devices in a mesh: section: 8 (over y, core), tile: 64 (over x, z).
Axes of the slice: x: 4, y: 4, z: 16, core: 2. Of those that a mesh axis runs over, the one named last changes fastest.
Arguments:
- latent_feat: bfloat16 [4096, 128, 256], P(('section', 'tile')), may hold values from -6 to 6
- reward_grad: bfloat16 [2048, 64, 192], P('section', 'tile'), may hold values from -6 to 6
- patches: bfloat16 [2048, 3072], P('section', 'tile'), may hold values from -1 to 1
- up_weight: bfloat16 [3, 3, 256, 256], replicated, may hold values from -0.125 to 0.125
- up_bias: float32 [256], replicated, may hold values from -3 to 3
- norm_gain: float32 [256], replicated, may hold values from 0.5 to 2
- norm_bias: float32 [256], replicated, may hold values from -3 to 3
- out_weight: bfloat16 [3, 3, 256, 3], replicated, may hold values from -1.25 to 1.25
- stem_weight: bfloat16 [48, 192], replicated, may hold values from -0.875 to 0.875
- stem_bias: float32 [192], replicated, may hold values from -4 to 4
- stem_gain: float32 [192], replicated, may hold values from 0.5 to 2
- tile_count: int32 [512], replicated, may hold values from 1 to 3, as said below
- tile_cols: int32 [512, 3], replicated, may hold values from 0 to 112, as said below
Outputs:
- latent_grad: bfloat16 [4096, 128, 256], P(('section', 'tile'))
Inputs may be any that keep to these rules, and one draw needn't show every extreme that they name: `tile_count`: each block has between 1 and 3 live tiles; some block has 3. `tile_cols`: slots k >= tile_count[b] are unused. Tiles of one block may cover the same columns.
All inputs are finite; a program needn't handle non-finite values.
Results may differ from a plain program's by a relative error of at most 0.0064.
Values may be sent and summed in bfloat16 or wider, within the bound.
A program may use at most 64 MiB of HBM per device.

v0:
```python
import jax
import jax.numpy as jnp
from jax import lax
from jax.sharding import PartitionSpec as P

GROUPS = 32
STEM = 192
PATCH = 4
PIX = 48
TL = 16
MARGIN = 4
CENTRE = 8
MAXT = 3
IMAGES = 1


EPS = 1e-06


def extended_2(block, sides, width):
    for axis, dim in sides:
        count = lax.axis_size(axis)
        forward = [(i, i + 1) for i in range(count - 1)]
        backward = [(target, source) for source, target in forward]
        low = lax.ppermute(
            lax.slice_in_dim(block, block.shape[dim] - width, None, axis=dim), axis, forward
        )
        high = lax.ppermute(lax.slice_in_dim(block, 0, width, axis=dim), axis, backward)
        block = jnp.concatenate([low, block, high], axis=dim)
    return block


def stem_backward(gradient, pixels, stem_weight, stem_bias, stem_gain):
    stem = jnp.dot(pixels, stem_weight, preferred_element_type=jnp.float32) + stem_bias
    centred = stem - jnp.mean(stem, axis=-1, keepdims=True)
    inverse = lax.rsqrt(jnp.mean(centred * centred, axis=-1, keepdims=True) + EPS)
    normed = centred * inverse
    scaled = gradient.astype(jnp.float32) * stem_gain
    stem_grad = (
        scaled
        - jnp.mean(scaled, axis=-1, keepdims=True)
        - normed * jnp.mean(scaled * normed, axis=-1, keepdims=True)
    ) * inverse
    stem_grad = stem_grad.astype(jnp.bfloat16)
    result = lax.dot_general(
        stem_grad, stem_weight, (((1,), (1,)), ((), ())), preferred_element_type=jnp.float32
    )
    return result.astype(jnp.bfloat16)


def to_pixels(rows):
    count = rows.shape[0]
    width = rows.shape[1] // PIX
    grid = rows.reshape(count, width, 3, PATCH, PATCH)
    return grid.transpose(2, 0, 3, 1, 4).reshape(3, count * PATCH, width * PATCH)


def window_columns(padded, offsets, span):
    return jnp.concatenate(
        [
            padded[top : top + span, left : left + span].reshape(span * span, -1)
            for top, left in offsets
        ],
        axis=1,
    )


def tile_backward(
    inputs, out_grad, forward_matrix, backward_matrix, out_matrix, up_bias, norm_gain, norm_bias
):
    span = 2 * inputs.shape[0]
    channels = inputs.shape[2]
    forward_offsets = [(shift_row, shift_col) for shift_row in range(3) for shift_col in range(3)]
    backward_offsets = [
        (2 - shift_row, 2 - shift_col) for shift_row in range(3) for shift_col in range(3)
    ]
    upsampled = jnp.repeat(jnp.repeat(inputs, 2, axis=0), 2, axis=1)
    padded = jnp.pad(upsampled, ((1, 1), (1, 1), (0, 0)))
    features = window_columns(padded, forward_offsets, span)
    preact = jnp.dot(features, forward_matrix, preferred_element_type=jnp.float32) + up_bias
    grouped = preact.reshape(span * span, GROUPS, channels // GROUPS)
    centred = grouped - jnp.mean(grouped, axis=(0, 2), keepdims=True)
    inverse = lax.rsqrt(jnp.mean(centred * centred, axis=(0, 2), keepdims=True) + EPS)
    normed = centred * inverse
    activated = normed.reshape(span * span, channels) * norm_gain + norm_bias
    grad_pad = jnp.pad(out_grad, ((0, 0), (1, 1), (1, 1)))
    out_columns = jnp.concatenate(
        [
            grad_pad[:, top : top + span, left : left + span].reshape(3, span * span)
            for top, left in backward_offsets
        ],
        axis=0,
    )
    act_grad = lax.dot_general(
        out_columns, out_matrix, (((0,), (0,)), ((), ())), preferred_element_type=jnp.float32
    )
    sigma = jax.nn.sigmoid(activated)
    norm_grad = act_grad * sigma * (1.0 + activated * (1.0 - sigma))
    scaled = (norm_grad * norm_gain).reshape(span * span, GROUPS, channels // GROUPS)
    pre_grad = (
        scaled
        - jnp.mean(scaled, axis=(0, 2), keepdims=True)
        - normed * jnp.mean(scaled * normed, axis=(0, 2), keepdims=True)
    ) * inverse
    pre_grad = pre_grad.reshape(span, span, channels).astype(jnp.bfloat16)
    grad_padded = jnp.pad(pre_grad, ((1, 1), (1, 1), (0, 0)))
    back_features = window_columns(grad_padded, backward_offsets, span)
    up_grad = jnp.dot(back_features, backward_matrix, preferred_element_type=jnp.float32)
    half = span // 2
    return up_grad.reshape(half, 2, half, 2, channels).sum(axis=(1, 3))


def add_block(total, piece, row, column):
    zero_index = jnp.zeros((), jnp.int32)
    current = lax.dynamic_slice(total, (row, column, zero_index), piece.shape)
    return lax.dynamic_update_slice(total, current + piece, (row, column, zero_index))


def per_device(
    latent_feat,
    reward_grad,
    patches,
    up_weight,
    up_bias,
    norm_gain,
    norm_bias,
    out_weight,
    stem_weight,
    stem_bias,
    stem_gain,
    tile_count,
    tile_cols,
):
    blocks = lax.axis_size("section") * lax.axis_size("tile")
    block = lax.axis_index(("section", "tile"))
    per_image = blocks // IMAGES
    keep_top = block % per_image != 0
    keep_bottom = block % per_image != per_image - 1
    width = latent_feat.shape[1]
    channels = latent_feat.shape[2]
    zero_index = jnp.zeros((), jnp.int32)
    local_rows = reward_grad.shape[0]
    local_cols = reward_grad.shape[1]
    pixel = stem_backward(
        reward_grad.reshape(local_rows * local_cols, STEM),
        patches,
        stem_weight,
        stem_bias,
        stem_gain,
    )
    arrived = lax.all_to_all(pixel, "tile", split_axis=0, concat_axis=1, tiled=True)
    image_grad = to_pixels(arrived)
    counted = lax.dynamic_index_in_dim(tile_count, block, 0, keepdims=False)
    own_columns = lax.dynamic_index_in_dim(tile_cols, block, 0, keepdims=False)
    forward_matrix = up_weight.reshape(9 * channels, channels)
    backward_matrix = up_weight.transpose(0, 1, 3, 2).reshape(9 * channels, channels)
    out_matrix = out_weight.transpose(0, 1, 3, 2).reshape(27, channels)
    extended = extended_2(latent_feat, ((("section", "tile"), 0),), MARGIN)
    extended = jnp.concatenate(
        [
            jnp.where(keep_top, extended[:MARGIN], 0.0),
            extended[MARGIN : MARGIN + CENTRE],
            jnp.where(keep_bottom, extended[MARGIN + CENTRE :], 0.0),
        ],
        axis=0,
    )

    def tile_input(anchor):
        return lax.dynamic_slice(extended, (zero_index, anchor, zero_index), (TL, TL, channels))

    gradients = []
    for slot in range(MAXT):
        anchor = own_columns[slot]

        def compute():
            centre = lax.dynamic_slice(
                image_grad,
                (zero_index, zero_index, 2 * anchor + 2 * MARGIN),
                (3, 2 * CENTRE, 2 * CENTRE),
            )
            out_grad = jnp.pad(centre, ((0, 0), (2 * MARGIN, 2 * MARGIN), (2 * MARGIN, 2 * MARGIN)))
            inputs = tile_input(anchor)
            return tile_backward(
                inputs,
                out_grad,
                forward_matrix,
                backward_matrix,
                out_matrix,
                up_bias,
                norm_gain,
                norm_bias,
            )

        def skipped():
            return jnp.zeros((TL, TL, channels), jnp.float32)

        gradients.append(lax.cond(slot < counted, compute, skipped))
    total = jnp.zeros((CENTRE, width, channels), jnp.float32)
    for slot in range(MAXT):
        total = add_block(
            total, gradients[slot][MARGIN : MARGIN + CENTRE], zero_index, own_columns[slot]
        )
    outgoing = jnp.zeros((2 * MARGIN, width, channels), jnp.float32)
    for slot in range(MAXT):
        outgoing = add_block(outgoing, gradients[slot][:MARGIN], zero_index, own_columns[slot])
        outgoing = add_block(
            outgoing, gradients[slot][TL - MARGIN :], zero_index + MARGIN, own_columns[slot]
        )
    returned = extended_2(
        outgoing.astype(jnp.bfloat16), ((("section", "tile"), 0),), MARGIN
    ).astype(outgoing.dtype)
    total = total + jnp.concatenate(
        [
            jnp.where(keep_top, returned[:MARGIN], 0.0),
            jnp.where(keep_bottom, returned[3 * MARGIN :], 0.0),
        ],
        axis=0,
    )
    return total.astype(jnp.bfloat16)


def solution(mesh):
    return jax.shard_map(
        per_device,
        mesh=mesh,
        in_specs=(
            P(("section", "tile"), None, None),
            P("section", "tile", None),
            P("section", "tile"),
            P(),
            P(),
            P(),
            P(),
            P(),
            P(),
            P(),
            P(),
            P(),
            P(),
        ),
        out_specs=P(("section", "tile"), None, None),
        check_vma=False,
    )
```

profile of v0, /device:TPU:110, one launch (start us, length us, event | category | flops | bytes accessed | tf_op | source)
XLA Modules:
  0.0 164.3 jit_solution(17148599520619447978)
XLA Ops:
  0.0 1.1 fusion.25
  1.2 2.0 %collective-permute-start.1 = (bf16[4,128,256]{2,1,0:T(8,128)(2,1)S(1)}, bf16[4,128,256]{2,1,0:T(8,128)(2,1)S(1)}, u32[]{:S(2)}, u32[]{:S(2)}) collective-permute-start(bf16[4,128,256]{2,1,0:T(8,128)(2,1)S(1)} %get-tuple-element.189), channel_id=1, source_target_pairs={{1,0},{2,1},{3,2},{4,3},{5,4},{6,5},{7,6},{8,7},{9,8},{10,9},{11,1... | collective-permute-start | bytes 786440 | tf_op jit(solution)/shard_map/ppermute | solution.py:28
  3.2 5.0 %collective-permute-start = (bf16[4,128,256]{2,1,0:T(8,128)(2,1)S(1)}, bf16[4,128,256]{2,1,0:T(8,128)(2,1)S(1)}, u32[]{:S(2)}, u32[]{:S(2)}) collective-permute-start(bf16[4,128,256]{2,1,0:T(8,128)(2,1)S(1)} %get-tuple-element.188), channel_id=1, source_target_pairs={{0,1},{1,2},{2,3},{3,4},{4,5},{5,6},{6,7},{7,8},{8,9},{9,10},{10,1... | collective-permute-start | bytes 786440 | tf_op jit(solution)/shard_map/ppermute | solution.py:25
  8.2 1.0 fusion.27
  9.3 1.0 fusion.12
  10.3 1.1 convolution_convert_fusion
  11.5 0.7 copy.19
  12.2 16.2 %all-to-all-start = ((bf16[64,4,48]{2,1,0:T(4,128)(2,1)}), bf16[64,4,48]{2,1,0:T(4,128)(2,1)S(1)}, u32[]{:S(2)}, u32[]{:S(2)}) async-start(bf16[64,4,48]{2,1,0:T(4,128)(2,1)} %bitcast.60), calls=%async_computation | async-start | bytes 131072 | tf_op jit(solution)/shard_map/all_to_all | solution.py:151
  28.5 0.8 constant_dynamic-slice_fusion.6
  29.2 0.6 fusion.26
  33.7 2.4 %copy.22 = bf16[3,3,256,256]{3,2,1,0:T(8,128)(2,1)} copy(bf16[3,3,256,256]{2,3,1,0:T(8,128)(2,1)} %bitcast.155) | data formatting | bytes 2359296 | tf_op jit(solution)/shard_map/transpose | solution.py:156
  36.1 1.3 dynamic_slice.47
  41.3 0.4 copy.21
  41.8 1.4 reshape.471
  43.3 1.1 pad_maximum_fusion
  44.4 26.8 %conditional.3 = (f32[16,16,256]{2,1,0:T(8,128)}) conditional(s32[]{:T(128)} %bitcast.57, () %tuple.23, (s32[]{:T(128)}, bf16[3,16,256]{2,1,0:T(8,128)(2,1)S(1)}, bf16[27,256]{1,0:T(8,128)(2,1)S(1)}, bf16[16,128,256]{2,1,0:T(8,128)(2,1)}, bf16[2304,256]{1,0:T(8,128)(2,1)}, /*index=5*/f32[256]{0:T(256)S(1)}, f32[256]{0:T(256)S(1)}, f32[256]{0:T(256)S(1)}, ...), branch_computations={%region_4.5_spmd, %region_5.15_spmd} | conditional | flops 2439446528 | bytes 66330808 | solution.py:197
  46.5 1.0 constant_dynamic-slice_fusion
  47.5 0.5 broadcast_in_dim.10
  48.2 0.5 pad_slice_fusion.8
  48.7 0.9 constant_dynamic-update-slice_fusion.8
  49.6 0.8 constant_dynamic-update-slice_fusion.7
  50.5 0.9 constant_dynamic-update-slice_fusion.6
  51.4 0.9 constant_dynamic-update-slice_fusion.5
  52.4 0.8 constant_dynamic-update-slice_fusion.4
  53.3 0.9 constant_dynamic-update-slice_fusion.3
  54.1 0.9 constant_dynamic-update-slice_fusion.2
  55.0 0.9 constant_dynamic-update-slice_fusion.1
  55.9 0.9 constant_dynamic-update-slice_fusion
  56.8 3.7 %fusion.21 = (f32[256]{0:T(256)S(1)}, f32[1024,256]{1,0:T(8,128)S(1)}) fusion(f32[256]{0:T(256)S(1)} %get-tuple-element.73, bf16[1024,2304]{1,0:T(8,128)(2,1)} %constant_dynamic-update-slice_fusion, bf16[2304,256]{1,0:T(8,128)(2,1)S(1)} %copy-done.3), kind=kOutput, calls=%fused_computation.206 | convolution fusion | flops 1208483584 | bytes 6948864 | tf_op jit(solution)/shard_map/cond/branch_1_fun/dot_general | solution.py:80
  63.6 0.7 fusion.18
  65.4 0.8 pad_slice_fusion
  66.9 0.7 copy-done.6
  67.6 1.4 fusion.28
  69.0 0.6 reshape.402
  69.6 1.6 reduce_sum.161
  71.2 0.8 slice.312
  72.1 1.6 slice.309
  74.0 0.9 slice_add_fusion.6
  75.9 0.7 conditional.5
  75.9 0.7 broadcast.255
  76.7 0.9 slice_add_fusion.3
  77.8 0.9 slice_add_fusion.2
  79.0 74.8 %collective-permute-start.2 = (bf16[4,128,256]{2,1,0:T(8,128)(2,1)S(1)}, bf16[4,128,256]{2,1,0:T(8,128)(2,1)S(1)}, u32[]{:S(2)}, u32[]{:S(2)}) collective-permute-start(bf16[4,128,256]{2,1,0:T(8,128)(2,1)S(1)} %get-tuple-element.186), channel_id=1, source_target_pairs={{0,1},{1,2},{2,3},{3,4},{4,5},{5,6},{6,7},{7,8},{8,9},{9,10},{10,1... | collective-permute-start | bytes 786440 | tf_op jit(solution)/shard_map/ppermute | solution.py:25
  153.8 1.9 %collective-permute-start.3 = (bf16[4,128,256]{2,1,0:T(8,128)(2,1)S(1)}, bf16[4,128,256]{2,1,0:T(8,128)(2,1)S(1)}, u32[]{:S(2)}, u32[]{:S(2)}) collective-permute-start(bf16[4,128,256]{2,1,0:T(8,128)(2,1)S(1)} %get-tuple-element.187), channel_id=1, source_target_pairs={{1,0},{2,1},{3,2},{4,3},{5,4},{6,5},{7,6},{8,7},{9,8},{10,9},{11,1... | collective-permute-start | bytes 786440 | tf_op jit(solution)/shard_map/ppermute | solution.py:28
  155.8 1.1 dynamic_update_slice.27
  157.3 0.9 slice_add_fusion
  158.5 4.8 %collective-permute-done.3 = bf16[4,128,256]{2,1,0:T(8,128)(2,1)S(1)} collective-permute-done((bf16[4,128,256]{2,1,0:T(8,128)(2,1)S(1)}, bf16[4,128,256]{2,1,0:T(8,128)(2,1)S(1)}, u32[]{:S(2)}, u32[]{:S(2)}) %collective-permute-start.3) | collective-permute-done | bytes 262176 | tf_op jit(solution)/shard_map/ppermute | solution.py:28
  163.4 0.9 fusion.9
  (94 shorter events, 7.5 us)
Async XLA Ops:
  0.0 8.2 %copy-start = (bf16[48,192]{1,0:T(8,128)(2,1)S(1)}, bf16[48,192]{1,0:T(8,128)(2,1)}, u32[]{:S(2)}) copy-start(bf16[48,192]{1,0:T(8,128)(2,1)} %param.27) | copy-start | bytes 55300
  0.0 43.3 %copy-start.2 = (bf16[8,128,256]{2,1,0:T(8,128)(2,1)S(1)}, bf16[8,128,256]{2,1,0:T(8,128)(2,1)}, u32[]{:S(2)}) copy-start(bf16[8,128,256]{2,1,0:T(8,128)(2,1)} %param.19) | copy-start | bytes 1572868
  0.0 36.1 %copy-start.9 = (bf16[3,3,256,3]{2,3,1,0:T(4,128)(2,1)S(1)}, bf16[3,3,256,3]{2,3,1,0:T(4,128)(2,1)}, u32[]{:S(2)}) copy-start(bf16[3,3,256,3]{2,3,1,0:T(4,128)(2,1)} %param.26) | copy-start | bytes 41476
  0.0 44.4 %copy-start.10 = (f32[256]{0:T(256)S(1)}, f32[256]{0:T(256)}, u32[]{:S(2)}) copy-start(f32[256]{0:T(256)} %param.23) | copy-start | bytes 3076
  0.0 44.4 %copy-start.11 = (f32[256]{0:T(256)S(1)}, f32[256]{0:T(256)}, u32[]{:S(2)}) copy-start(f32[256]{0:T(256)} %param.24) | copy-start | bytes 3076
  0.0 44.4 %copy-start.12 = (f32[256]{0:T(256)S(1)}, f32[256]{0:T(256)}, u32[]{:S(2)}) copy-start(f32[256]{0:T(256)} %param.25) | copy-start | bytes 3076
  1.2 42.0 %collective-permute-start.1 = (bf16[4,128,256]{2,1,0:T(8,128)(2,1)S(1)}, bf16[4,128,256]{2,1,0:T(8,128)(2,1)S(1)}, u32[]{:S(2)}, u32[]{:S(2)}) collective-permute-start(bf16[4,128,256]{2,1,0:T(8,128)(2,1)S(1)} %get-tuple-element.189), channel_id=1, source_target_pairs={{1,0},{2,1},{3,2},{4,3},{5,4},{6,5},{7,6},{8,7},{9,8},{10,9},{11,1... | collective-permute-start | bytes 786440 | tf_op jit(solution)/shard_map/ppermute | solution.py:28
  3.2 40.1 %collective-permute-start = (bf16[4,128,256]{2,1,0:T(8,128)(2,1)S(1)}, bf16[4,128,256]{2,1,0:T(8,128)(2,1)S(1)}, u32[]{:S(2)}, u32[]{:S(2)}) collective-permute-start(bf16[4,128,256]{2,1,0:T(8,128)(2,1)S(1)} %get-tuple-element.188), channel_id=1, source_target_pairs={{0,1},{1,2},{2,3},{3,4},{4,5},{5,6},{6,7},{7,8},{8,9},{9,10},{10,1... | collective-permute-start | bytes 786440 | tf_op jit(solution)/shard_map/ppermute | solution.py:25
  12.2 29.0 %all-to-all-start = ((bf16[64,4,48]{2,1,0:T(4,128)(2,1)}), bf16[64,4,48]{2,1,0:T(4,128)(2,1)S(1)}, u32[]{:S(2)}, u32[]{:S(2)}) async-start(bf16[64,4,48]{2,1,0:T(4,128)(2,1)} %bitcast.60), calls=%async_computation | async-start | bytes 131072 | tf_op jit(solution)/shard_map/all_to_all | solution.py:151
  52.4 4.4 %copy-start.3 = (bf16[2304,256]{1,0:T(8,128)(2,1)S(1)}, bf16[2304,256]{1,0:T(8,128)(2,1)}, u32[]{:S(2)}) copy-start(bf16[2304,256]{1,0:T(8,128)(2,1)} %get-tuple-element.72) | copy-start | bytes 3538948 | tf_op jit(solution)/shard_map/cond
  66.3 1.3 copy-start.6
  78.6 85.7 %copy-start.1 = (bf16[48,192]{1,0:T(8,128)(2,1)S(1)}, bf16[48,192]{1,0:T(8,128)(2,1)}, u32[]{:S(2)}) copy-start(bf16[48,192]{1,0:T(8,128)(2,1)} %param.27) | copy-start | bytes 55300
  79.0 79.5 %collective-permute-start.2 = (bf16[4,128,256]{2,1,0:T(8,128)(2,1)S(1)}, bf16[4,128,256]{2,1,0:T(8,128)(2,1)S(1)}, u32[]{:S(2)}, u32[]{:S(2)}) collective-permute-start(bf16[4,128,256]{2,1,0:T(8,128)(2,1)S(1)} %get-tuple-element.186), channel_id=1, source_target_pairs={{0,1},{1,2},{2,3},{3,4},{4,5},{5,6},{6,7},{7,8},{8,9},{9,10},{10,1... | collective-permute-start | bytes 786440 | tf_op jit(solution)/shard_map/ppermute | solution.py:25
  153.8 9.5 %collective-permute-start.3 = (bf16[4,128,256]{2,1,0:T(8,128)(2,1)S(1)}, bf16[4,128,256]{2,1,0:T(8,128)(2,1)S(1)}, u32[]{:S(2)}, u32[]{:S(2)}) collective-permute-start(bf16[4,128,256]{2,1,0:T(8,128)(2,1)S(1)} %get-tuple-element.187), channel_id=1, source_target_pairs={{1,0},{2,1},{3,2},{4,3},{5,4},{6,5},{7,6},{8,7},{9,8},{10,9},{11,1... | collective-permute-start | bytes 786440 | tf_op jit(solution)/shard_map/ppermute | solution.py:28
where the time goes:
time: 166 us; the launch traced here: 164 us
  starting transfers between devices  100 us (60%)
  local copies, waits for them, and re-layouts  30.6 us (18%)
  other arithmetic  9.79 us (6%)
  between operations  8.01 us (5%)
  matrix products  7.97 us (5%)
  waiting for transfers between devices  4.78 us (3%)
  loops' own time  3.22 us (2%)
    ppermute x2, starting transfers between devices, extended_2(): lax.ppermute(lax.slice_in_dim(block, block.shape[dim] - width, None, axis...  79.8 us
    all_to_all x1, starting transfers between devices, per_device(): lax.all_to_all(pixel, 'tile', split_axis=0, concat_axis=1, tiled=True)  16.2 us
    cond x19, local copies, waits for them, and re-layouts  7.87 us
    ppermute x2, waiting for transfers between devices, extended_2(): lax.ppermute(lax.slice_in_dim(block, 0, width, axis=dim), axis, backward)  4.77 us
    ppermute x2, starting transfers between devices, extended_2(): lax.ppermute(lax.slice_in_dim(block, 0, width, axis=dim), axis, backward)  3.94 us
    dot_general x1, matrix products, tile_backward(): jnp.dot(features, forward_matrix, preferred_element_type=jnp.float32)  3.73 us
    add x7, other arithmetic, add_block(): current + piece  3.59 us
  transfers between devices with their start and end apart: 5, of which 1 were waited for; matrix products, arithmetic and copies ran while one was open for 8% of the time, Pallas kernels for 0%

commit v1 on v0

v1 whole, which is shorter than its diff:
```python
import functools

import jax
import jax.numpy as jnp
import numpy as np
from jax import lax
from jax.experimental import pallas as pl
from jax.experimental.pallas import tpu as pltpu
from jax.sharding import PartitionSpec as P

EPS = 1e-06
CH = 256
STEM = 192
PIX = 48
TL = 16
SLOTS = 3
LINE = SLOTS * TL
NZ = 16
F32 = jnp.float32
BF16 = jnp.bfloat16
MESH = pl.DeviceIdType.MESH
NT = (((1,), (1,)), ((), ()))
TN = (((0,), (0,)), ((), ()))
(
    LATENT,
    REWARD,
    PIXELS,
    UP_WEIGHT,
    UP_BIAS,
    NORM_GAIN,
    NORM_BIAS,
    OUT_WEIGHT,
    STEM_WEIGHT,
    STEM_BIAS,
    STEM_GAIN,
    TILE_COUNT,
    TILE_COLS,
    TAPS_TABLE,
    LANES_TABLE,
) = range(15)
OPERANDS = 15
STEM_LOADS = (PIXELS, STEM_WEIGHT, STEM_BIAS, REWARD, STEM_GAIN)
OTHER_LOADS = (
    TILE_COLS,
    TILE_COUNT,
    LATENT,
    UP_WEIGHT,
    UP_BIAS,
    NORM_GAIN,
    NORM_BIAS,
    OUT_WEIGHT,
    TAPS_TABLE,
    LANES_TABLE,
)
TAPS = {(0, 0): (0,), (0, 1): (1, 2), (1, 0): (0, 1), (1, 1): (2,)}


def out_taps():
    table = np.zeros((4, 128, 128), np.float32)
    for r in range(2):
        for s in range(2):
            for di in range(3):
                for dj in range(3):
                    for c in range(3):
                        for y in range(2):
                            for x in range(2):
                                a = r + 1 - (2 * (di - 1) + y)
                                e = s + 1 - (2 * (dj - 1) + x)
                                if 0 <= a < 3 and 0 <= e < 3:
                                    lane = (di * 3 + dj) * 12 + c * 4 + y * 2 + x
                                    table[r * 2 + s, lane, (a * 3 + e) * 8 + c] = 1
    return table.reshape(512, 128)


def cell_lanes():
    table = np.zeros((128, 2, 2, 128), np.float32)
    for c in range(3):
        for dy in range(4):
            for dx in range(4):
                for copy in range(9):
                    lane = copy * 12 + c * 4 + (dy % 2) * 2 + dx % 2
                    table[c * 16 + dy * 4 + dx, dx // 2, dy // 2, lane] = 1
    return table.reshape(128, 512)


def iota(shape, axis):
    return lax.broadcasted_iota(jnp.int32, shape, axis)


def dot(a, b):
    return jnp.dot(a, b, preferred_element_type=F32)


def three_rows(row):
    high = row.astype(BF16).astype(F32)
    rest = row - high
    middle = rest.astype(BF16).astype(F32)
    low = rest - middle
    at = iota((16, row.shape[1]), 0)
    rows = jnp.where(at == 0, high, jnp.where(at == 1, middle, jnp.where(at == 2, low, 0.0)))
    return rows.astype(BF16)


def kernel(nx, sections, *refs):
    operands, out, scratch = refs[:OPERANDS], refs[OPERANDS], refs[OPERANDS + 1 :]
    copies, scratch = scratch[:OPERANDS], scratch[OPERANDS:]
    (
        latent,
        reward,
        pixels,
        up_weight,
        up_bias,
        norm_gain,
        norm_bias,
        out_weight,
        stem_weight,
        stem_bias,
        stem_gain,
        tile_count,
        tile_cols,
        taps,
        lanes,
    ) = copies
    (
        wide,
        combined,
        out_matrix,
        out_rows,
        margin_send,
        margin_recv,
        image,
        x_recv,
        z_send,
        z_recv,
        preact,
        slopes,
        grads,
        zgrad,
        cells,
        own_grad,
        grad_send,
        grad_recv,
        groups,
        load_sem,
        msend_sem,
        mrecv_sem,
        xsend_sem,
        xrecv_sem,
        zsend_sem,
        zrecv_sem,
        gsend_sem,
        grecv_sem,
    ) = scratch
    tiles = nx * NZ
    blocks = sections * tiles
    section = lax.axis_index("section")
    tile = lax.axis_index("tile")
    mx = lax.div(tile, NZ)
    mz = lax.rem(tile, NZ)
    block = section * tiles + tile
    before = lax.rem(block + blocks - 1, blocks)
    after = lax.rem(block + 1, blocks)

    def device(index):
        return (lax.div(index, tiles), lax.rem(index, tiles))

    def along_x(index):
        return (section, index * NZ + mz)

    def along_z(index):
        return (section, mx * NZ + index)

    barrier = pltpu.get_barrier_semaphore()

    def greet(target):
        pl.semaphore_signal(barrier, inc=1, device_id=target, device_id_type=MESH)

    def load(n):
        return pltpu.make_async_copy(operands[n], copies[n], load_sem.at[n])

    for n in STEM_LOADS:
        load(n).start()

    def greet_z(d, carry):
        greet(along_z(lax.rem(mz + d, NZ)))
        return carry

    lax.fori_loop(1, NZ, greet_z, 0)
    for d in range(1, nx):
        greet(along_x(lax.rem(mx + d, nx)))
    greet(device(before))
    greet(device(after))
    for n in OTHER_LOADS:
        load(n).start()

    row_at = iota((CH, CH), 0)
    col_at = iota((CH, CH), 1)
    groups[...] = ((row_at >> 3) == (col_at >> 3)).astype(F32).astype(BF16)
    zeros = jnp.zeros((LINE, 4 * CH), BF16)
    zgrad[0:LINE, :] = zeros
    zgrad[17 * LINE : 18 * LINE, :] = zeros
    wide[0:LINE, :] = zeros[:, : 3 * CH]
    wide[17 * LINE : 18 * LINE, :] = zeros[:, : 3 * CH]
    out_rows[...] = jnp.zeros_like(out_rows)
    reorder = (col_at == ((row_at >> 2) & 3) * (NZ * 4) + (row_at >> 4) * 4 + (row_at & 3)).astype(
        F32
    ).astype(BF16)
    shift_low = ((col_at == row_at - 1) & ((row_at & 15) != 0)).astype(F32).astype(BF16)
    shift_high = ((col_at == row_at + 1) & ((row_at & 15) != 15)).astype(F32).astype(BF16)
    keep_before = block != 0
    keep_after = block != blocks - 1

    ones = jnp.ones((16, CH), BF16)

    def column_of(row):
        return lax.dot_general(three_rows(row), ones, TN, preferred_element_type=F32)

    for n in STEM_LOADS:
        load(n).wait()
    weight = stem_weight[...]
    stem = lax.dot_general(weight, pixels[...], TN, preferred_element_type=F32) + column_of(
        stem_bias[...]
    )
    centred = stem - jnp.mean(stem, axis=0, keepdims=True)
    inverse = lax.rsqrt(jnp.mean(centred * centred, axis=0, keepdims=True) + EPS)
    normed = centred * inverse
    scaled = reward[...].astype(F32) * column_of(stem_gain[...])
    stem_grad = (
        scaled
        - jnp.mean(scaled, axis=0, keepdims=True)
        - normed * jnp.mean(scaled * normed, axis=0, keepdims=True)
    ) * inverse
    padded_weight = jnp.concatenate([weight, jnp.zeros((128 - PIX, STEM), BF16)], axis=0)
    pixel_grad = dot(padded_weight, stem_grad.astype(BF16))
    image[...] = pixel_grad.T.astype(BF16).reshape(nx, NZ * 4, 128)
    x_recv[pl.ds(mx, 1)] = image[pl.ds(mx, 1)]

    pl.semaphore_wait(barrier, 2 + (nx - 1) + (NZ - 1))

    def x_copy(d, slot):
        target = lax.rem(mx + d, nx)
        return pltpu.make_async_remote_copy(
            src_ref=image.at[target],
            dst_ref=x_recv.at[slot],
            send_sem=xsend_sem.at[d - 1],
            recv_sem=xrecv_sem.at[d - 1],
            device_id=along_x(target),
            device_id_type=MESH,
        )

    for d in range(1, nx):
        x_copy(d, mx).start()

    at3 = iota((SLOTS, blocks), 1)
    at1 = iota((1, blocks), 1)
    for n in (TILE_COLS, TILE_COUNT, LATENT):
        load(n).wait()
    all_cols = tile_cols[...].astype(F32)
    all_counts = tile_count[...].astype(F32)

    def columns(index):
        return jnp.sum(jnp.where(at3 == index, all_cols, 0.0), axis=1, keepdims=True)

    def count(index):
        return jnp.sum(jnp.where(at1 == index, all_counts, 0.0), axis=1, keepdims=True)

    cols_own, cols_before, cols_after = columns(block), columns(before), columns(after)

    def slot_rows(cols, width):
        return jnp.concatenate(
            [jnp.broadcast_to(cols[k : k + 1, :], (TL, width)) for k in range(SLOTS)], axis=0
        )

    place = (iota((LINE, 128), 0) & 15).astype(F32)
    lane_f = iota((LINE, 128), 1).astype(F32)

    def gather_rows(cols):
        return (lane_f == slot_rows(cols, 128) + place).astype(F32)

    pick_own = gather_rows(cols_own)
    pick_up = jnp.concatenate([pick_own, gather_rows(cols_before)], axis=0).astype(BF16)
    pick_down = jnp.concatenate([pick_own, gather_rows(cols_after)], axis=0).astype(BF16)
    for r in range(8):
        side = r // 4
        rows = dot(pick_down if side else pick_up, latent[r]).astype(BF16)
        wide[(5 + r) * LINE : (6 + r) * LINE, CH : 2 * CH] = rows[0:LINE]
        margin_send[side, (r % 4) * LINE : (r % 4 + 1) * LINE, :] = rows[LINE : 2 * LINE]

    def margin_copy(side, target):
        return pltpu.make_async_remote_copy(
            src_ref=margin_send.at[side],
            dst_ref=margin_recv.at[1 - side],
            send_sem=msend_sem.at[side],
            recv_sem=mrecv_sem.at[1 - side],
            device_id=target,
            device_id_type=MESH,
        )

    margin_copy(0, device(before)).start()
    margin_copy(1, device(after)).start()

    load(UP_WEIGHT).wait()
    for r in range(2):
        for s in range(2):
            for t in range(2):
                for v in range(2):
                    total = None
                    for a in TAPS[r, t]:
                        for e in TAPS[s, v]:
                            term = up_weight[a, e].astype(F32)
                            total = term if total is None else total + term
                    at = (t * 2 + v) * CH
                    combined[r * 2 + s, at : at + CH, :] = total.astype(BF16)

    for n in (UP_BIAS, NORM_GAIN, NORM_BIAS, OUT_WEIGHT, TAPS_TABLE, LANES_TABLE):
        load(n).wait()
    for ae in range(9):
        out_rows[ae * 8 : ae * 8 + 3, :] = out_weight[ae].astype(F32)
    flat_taps = out_rows[...].astype(BF16)
    for ph in range(4):
        out_matrix[:, ph * CH : (ph + 1) * CH] = dot(
            taps[ph * 128 : (ph + 1) * 128, :], flat_taps
        ).astype(BF16)

    source = iota((1, 512), 1)
    source_row = source & 3
    source_x = (source >> 2) & 3
    source_z = (source >> 4) & 15
    cell_of = 2 * (source_x * NZ + source_z) + (source >> 8)
    source_key = (cell_of + 1000 * source_row).astype(F32)
    own_rows = slot_rows(cols_own, 512)
    place_wide = (iota((LINE, 512), 0) & 15).astype(F32)
    inside = (place_wide >= 4.0) & (place_wide < 12.0)
    choose = jnp.concatenate(
        [
            (jnp.where(inside, own_rows + place_wide + 1000.0 * pr, -1.0) == source_key)
            .astype(F32)
            .astype(BF16)
            for pr in range(4)
        ],
        axis=0,
    )

    lane = iota((128, 128), 1)
    column = iota((128, 128), 0).astype(F32)
    slot_of = lane >> 4
    offset_of = (lane & 15).astype(F32)

    def place_columns(cols, live, first_slot):
        start = jnp.where(
            slot_of == first_slot,
            jnp.broadcast_to(cols[0:1, :], (128, 128)),
            jnp.where(
                slot_of == first_slot + 1,
                jnp.broadcast_to(cols[1:2, :], (128, 128)),
                jnp.broadcast_to(cols[2:3, :], (128, 128)),
            ),
        )
        relative = (slot_of - first_slot).astype(F32)
        valid = (relative >= 0.0) & (relative < live) & (relative < float(SLOTS))
        return jnp.where(valid & (column == start + offset_of), 1.0, 0.0)

    none = jnp.zeros((1, 1), F32)
    own_place = place_columns(cols_own, count(block), 0)
    up_place = (
        own_place
        + place_columns(cols_before, jnp.where(keep_before, count(before), none), SLOTS)
    ).astype(BF16)
    down_place = (
        own_place + place_columns(cols_after, jnp.where(keep_after, count(after), none), SLOTS)
    ).astype(BF16)

    for d in range(1, nx):
        x_copy(d, lax.rem(mx + nx - d, nx)).wait_recv()
    by_z = dot(reorder, x_recv[...].reshape(nx * NZ * 4, 128)).astype(BF16)
    z_send[...] = by_z.reshape(NZ, nx * 4, 128)

    def z_copy(d, slot):
        target = lax.rem(mz + d, NZ)
        return pltpu.make_async_remote_copy(
            src_ref=z_send.at[target],
            dst_ref=z_recv.at[slot],
            send_sem=zsend_sem.at[d - 1],
            recv_sem=zrecv_sem.at[d - 1],
            device_id=along_z(target),
            device_id_type=MESH,
        )

    def z_start(n, carry):
        z_copy(1 + lax.rem(n + NZ // 2 - 1, NZ - 1), mz).start()
        return carry

    lax.fori_loop(0, NZ - 1, z_start, 0)
    z_recv[pl.ds(mz, 1)] = z_send[pl.ds(mz, 1)]

    margin_copy(0, device(before)).wait_recv()
    margin_copy(1, device(after)).wait_recv()
    top = margin_recv[0]
    bottom = margin_recv[1]
    wide[LINE : 5 * LINE, CH : 2 * CH] = jnp.where(keep_before, top, jnp.zeros_like(top))
    wide[13 * LINE : 17 * LINE, CH : 2 * CH] = jnp.where(
        keep_after, bottom, jnp.zeros_like(bottom)
    )
    for part in range(SLOTS):
        here = slice(LINE + part * CH, LINE + (part + 1) * CH)
        inputs = wide[here, CH : 2 * CH]
        wide[here, 0:CH] = dot(shift_low, inputs).astype(BF16)
        wide[here, 2 * CH : 3 * CH] = dot(shift_high, inputs).astype(BF16)

    bias = up_bias[...]
    total = jnp.zeros((LINE, CH), F32)
    for ph in range(4):
        r, s = ph // 2, ph % 2
        features = jnp.concatenate(
            [
                wide[(r + t) * LINE : (r + t + TL) * LINE, s * CH : (s + 2) * CH]
                for t in range(2)
            ],
            axis=1,
        )
        value = dot(features, combined[ph]) + bias
        preact[ph] = value
        total = total + jnp.sum(value.reshape(TL, LINE, CH), axis=0)

    def group_means(sums):
        rows = []
        for term in sums:
            high = term.astype(BF16).astype(F32)
            rest = term - high
            middle = rest.astype(BF16).astype(F32)
            rows += [high, middle, rest - middle]
        grouped = dot(jnp.concatenate(rows, axis=0).astype(BF16), groups[...])
        means = []
        for n in range(len(sums)):
            first = grouped[3 * n * LINE : (3 * n + 1) * LINE]
            second = grouped[(3 * n + 1) * LINE : (3 * n + 2) * LINE]
            third = grouped[(3 * n + 2) * LINE : (3 * n + 3) * LINE]
            line = (first + second + third) * (1.0 / 8192.0)
            means.append(
                jnp.concatenate(
                    [
                        jnp.broadcast_to(
                            jnp.sum(line[k * TL : (k + 1) * TL], axis=0, keepdims=True), (TL, CH)
                        )
                        for k in range(SLOTS)
                    ],
                    axis=0,
                )
            )
        return means

    (mean,) = group_means([total])

    def centre_rows(n, square):
        for step in range(4):
            at = pl.ds(pl.multiple_of((n * 4 + step) * LINE, LINE), LINE)
            for ph in range(4):
                off = preact[ph, at, :] - mean
                preact[ph, at, :] = off
                square = square + off * off
        return square

    square = lax.fori_loop(0, 4, centre_rows, jnp.zeros((LINE, CH), F32))
    (variance,) = group_means([square])
    inv = lax.rsqrt(variance + EPS)
    gain = jnp.broadcast_to(norm_gain[...], (LINE, CH))
    shift = jnp.broadcast_to(norm_bias[...], (LINE, CH))
    inv_gain = inv * gain

    def silu_slopes(n, carry):
        for ph in range(4):
            at = pl.ds(pl.multiple_of((n + 3) * LINE, LINE), LINE)
            value = preact[ph, at, :] * inv_gain + shift
            sigma = 0.5 * jnp.tanh(0.5 * value) + 0.5
            slopes[ph, pl.ds(pl.multiple_of(n * LINE, LINE), LINE), :] = (
                sigma * (1.0 + value * (1.0 - sigma)) * gain
            )
        return carry

    lax.fori_loop(0, 10, silu_slopes, 0)

    def z_wait(d, carry):
        z_copy(d, lax.rem(mz + NZ - d, NZ)).wait_recv()
        return carry

    lax.fori_loop(1, NZ, z_wait, 0)
    spread = dot(z_recv[...].reshape(NZ * nx * 4, 128), lanes[...]).astype(BF16)
    stacked = jnp.concatenate([spread[:, 0:256], spread[:, 256:512]], axis=0)
    found = dot(choose, stacked)
    lane_wide = iota((1, 256), 1) & 127
    copy_wide = sum([(lane_wide >= 12 * c).astype(jnp.int32) for c in range(1, 9)])
    col_wide = copy_wide - 3 * (
        (copy_wide >= 3).astype(jnp.int32) + (copy_wide >= 6).astype(jnp.int32)
    )
    copy_one = copy_wide[:, 0:128]
    low = pltpu.roll(found, 1, 0)
    high = pltpu.roll(found, 4 * LINE - 1, 0)
    merged = jnp.where(col_wide == 0, low, jnp.where(col_wide == 1, found, high))
    lines = []
    for pr in range(4):
        line = merged[pr * LINE : (pr + 1) * LINE]
        lines += [line[:, 0:128], line[:, 128:256]]
    nothing = jnp.zeros((LINE, 128), F32)

    def line_at(index):
        return lines[index] if 0 <= index < 8 else nothing

    for i in range(3, 13):
        around = jnp.where(
            copy_one < 3, line_at(i - 5), jnp.where(copy_one < 6, line_at(i - 4), line_at(i - 3))
        )
        cells[(i - 3) * LINE : (i - 2) * LINE, :] = around.astype(BF16)

    first = jnp.zeros((LINE, CH), F32)
    second = jnp.zeros((LINE, CH), F32)
    for ph in range(4):
        act = dot(cells[...], out_matrix[:, ph * CH : (ph + 1) * CH])
        for n in range(10):
            at = slice(n * LINE, (n + 1) * LINE)
            grad = act[at] * slopes[ph, at, :]
            grads[ph, at, :] = grad
            first = first + grad
            second = second + grad * preact[ph, (n + 3) * LINE : (n + 4) * LINE, :]
    first, second = group_means([first, second])
    offset = first * inv
    slope = second * inv * inv * inv

    def normal_grad(i):
        for ph in range(4):
            value = -offset - preact[ph, i * LINE : (i + 1) * LINE, :] * slope
            if 3 <= i < 13:
                value = value + grads[ph, (i - 3) * LINE : (i - 2) * LINE, :] * inv
            zgrad[(i + 1) * LINE : (i + 2) * LINE, ph * CH : (ph + 1) * CH] = value.astype(BF16)

    def input_grad(pieces):
        parts = []
        for pairs in (((0, 0),), ((0, 1), (1, 0)), ((1, 1),)):
            left, right = [], []
            for s, v in pairs:
                for r in range(2):
                    for t in range(2):
                        ph = r * 2 + s
                        rows = [
                            zgrad[
                                (i + 2 - r - t) * LINE : (i + 2 - r - t + lines_of) * LINE,
                                ph * CH : (ph + 1) * CH,
                            ]
                            for i, lines_of in pieces
                        ]
                        left.append(rows[0] if len(rows) == 1 else jnp.concatenate(rows, axis=0))
                        right.append(combined[ph, (t * 2 + v) * CH : (t * 2 + v + 1) * CH, :])
            parts.append(
                lax.dot_general(
                    jnp.concatenate(left, axis=1),
                    jnp.concatenate(right, axis=1),
                    NT,
                    preferred_element_type=F32,
                )
            )
        size = parts[0].shape[0]
        place_rows = iota((size, CH), 0) & 15
        return (
            parts[1]
            + jnp.where(place_rows < 15, pltpu.roll(parts[0], size - 1, 0), 0.0)
            + jnp.where(place_rows > 0, pltpu.roll(parts[2], 1, 0), 0.0)
        ).astype(BF16)

    def grad_copy(side, target):
        return pltpu.make_async_remote_copy(
            src_ref=grad_send.at[side],
            dst_ref=grad_recv.at[1 - side],
            send_sem=gsend_sem.at[side],
            recv_sem=grecv_sem.at[1 - side],
            device_id=target,
            device_id_type=MESH,
        )

    for i in (0, 1, 2, 3, 4, 11, 12, 13, 14, 15):
        normal_grad(i)
    margin_grad = input_grad(((0, 4), (12, 4)))
    grad_send[0] = margin_grad[0 : 4 * LINE]
    grad_send[1] = margin_grad[4 * LINE : 8 * LINE]
    grad_copy(0, device(before)).start()
    grad_copy(1, device(after)).start()
    for i in range(5, 11):
        normal_grad(i)
    own_grad[...] = input_grad(((4, 8),))

    grad_copy(0, device(before)).wait_recv()
    grad_copy(1, device(after)).wait_recv()
    rest = jnp.zeros((128 - 2 * LINE, CH), BF16)
    for r in range(8):
        side = r // 4
        at = (r % 4) * LINE
        terms = jnp.concatenate(
            [
                own_grad[r * LINE : (r + 1) * LINE, :],
                grad_recv[side, at : at + LINE, :],
                rest,
            ],
            axis=0,
        )
        out[r] = dot(down_place if side else up_place, terms).astype(BF16)

    margin_copy(0, device(before)).wait_send()
    margin_copy(1, device(after)).wait_send()
    for d in range(1, nx):
        x_copy(d, mx).wait_send()

    def z_sent(d, carry):
        z_copy(d, mz).wait_send()
        return carry

    lax.fori_loop(1, NZ, z_sent, 0)
    grad_copy(0, device(before)).wait_send()
    grad_copy(1, device(after)).wait_send()


def per_device(
    latent_feat,
    reward_grad,
    patches,
    up_weight,
    up_bias,
    norm_gain,
    norm_bias,
    out_weight,
    stem_weight,
    stem_bias,
    stem_gain,
    tile_count,
    tile_cols,
):
    sections = lax.axis_size("section")
    nx = lax.axis_size("tile") // NZ
    blocks = sections * nx * NZ
    operands = (
        latent_feat,
        reward_grad.reshape(-1, STEM).T,
        patches.T,
        up_weight,
        up_bias.reshape(1, CH),
        norm_gain.reshape(1, CH),
        norm_bias.reshape(1, CH),
        out_weight.transpose(0, 1, 3, 2).reshape(9, 3, CH),
        stem_weight,
        stem_bias.reshape(1, STEM),
        stem_gain.reshape(1, STEM),
        tile_count.reshape(1, blocks),
        tile_cols.T,
        jnp.asarray(out_taps(), BF16),
        jnp.asarray(cell_lanes(), BF16),
    )
    pinned = [pltpu.with_memory_space_constraint(array, pltpu.HBM) for array in operands]
    return pl.pallas_call(
        functools.partial(kernel, nx, sections),
        out_shape=pltpu.VMEM(latent_feat.shape, BF16),
        in_specs=[pl.BlockSpec(memory_space=pltpu.HBM)] * OPERANDS,
        out_specs=pl.BlockSpec(memory_space=pltpu.VMEM),
        scratch_shapes=[pltpu.VMEM(array.shape, array.dtype) for array in operands]
        + [
            pltpu.VMEM((18 * LINE, 3 * CH), BF16),
            pltpu.VMEM((4, 4 * CH, CH), BF16),
            pltpu.VMEM((128, 4 * CH), BF16),
            pltpu.VMEM((128, CH), F32),
            pltpu.VMEM((2, 4 * LINE, CH), BF16),
            pltpu.VMEM((2, 4 * LINE, CH), BF16),
            pltpu.VMEM((nx, NZ * 4, 128), BF16),
            pltpu.VMEM((nx, NZ * 4, 128), BF16),
            pltpu.VMEM((NZ, nx * 4, 128), BF16),
            pltpu.VMEM((NZ, nx * 4, 128), BF16),
            pltpu.VMEM((4, TL * LINE, CH), F32),
            pltpu.VMEM((4, 10 * LINE, CH), F32),
            pltpu.VMEM((4, 10 * LINE, CH), F32),
            pltpu.VMEM((18 * LINE, 4 * CH), BF16),
            pltpu.VMEM((10 * LINE, 128), BF16),
            pltpu.VMEM((8 * LINE, CH), BF16),
            pltpu.VMEM((2, 4 * LINE, CH), BF16),
            pltpu.VMEM((2, 4 * LINE, CH), BF16),
            pltpu.VMEM((CH, CH), BF16),
            pltpu.SemaphoreType.DMA((OPERANDS,)),
            pltpu.SemaphoreType.DMA((2,)),
            pltpu.SemaphoreType.DMA((2,)),
            pltpu.SemaphoreType.DMA((nx - 1,)),
            pltpu.SemaphoreType.DMA((nx - 1,)),
            pltpu.SemaphoreType.DMA((NZ - 1,)),
            pltpu.SemaphoreType.DMA((NZ - 1,)),
            pltpu.SemaphoreType.DMA((2,)),
            pltpu.SemaphoreType.DMA((2,)),
        ],
        compiler_params=pltpu.CompilerParams(
            collective_id=0, has_side_effects=True, vmem_limit_bytes=48 * 1024 * 1024
        ),
    )(*pinned)


def solution(mesh):
    return jax.shard_map(
        per_device,
        mesh=mesh,
        in_specs=(
            P(("section", "tile"), None, None),
            P("section", "tile", None),
            P("section", "tile"),
        )
        + (P(),) * 10,
        out_specs=P(("section", "tile"), None, None),
        check_vma=False,
    )
```

time: 166 us -> 36.5 us (0.22)
  the two profiles are of different devices: /device:TPU:110 before, /device:TPU:1 now
where the time goes in v1:
time: 36.5 us; the launch traced here: 36.3 us
  Pallas kernels  35.5 us (97%)
  local copies, waits for them, and re-layouts  0.8 us (2%)
    pallas_call x1, Pallas kernels, per_device(): pl.pallas_call(functools.partial(kernel, nx, sections), out_shape=pltpu.V...  35.5 us
    unnamed x1, local copies, waits for them, and re-layouts  0.8 us

profile of v1, /device:TPU:1, one launch (start us, length us, event | category | flops | bytes accessed | tf_op | source)
XLA Modules:
  0.0 36.3 jit_solution(12079231663093315626)
XLA Ops:
  0.0 35.5 %shard_map.145 = bf16[8,128,256]{2,1,0:T(8,128)(2,1)S(1)} custom-call(bf16[8,128,256]{2,1,0:T(8,128)(2,1)} %refs_0_.1, bf16[192,256]{1,0:T(8,128)(2,1)} %bitcast.14, bf16[48,256]{1,0:T(8,128)(2,1)} %bitcast.15, bf16[3,3,256,256]{3,2,1,0:T(8,128)(2,1)} %refs_3_.1, f32[1,256]{1,0:T(1,128)} %bitcast.19, f32[1,256]{1,0:T(1,128)} %bitcast.20, f32[1,256]{1,0:T(1,128)} %bitcast.21, ...), custom_call_target="tpu_custom_call" | custom-call | tf_op jit(solution)/shard_map/pallas_call | solution.py:655
  35.5 0.8 %copy.17 = bf16[8,128,256]{2,1,0:T(8,128)(2,1)} copy(bf16[8,128,256]{2,1,0:T(8,128)(2,1)S(1)} %shard_map.145) | data formatting | bytes 1048576

commit v2 on v1

--- a/solution.py
+++ b/solution.py
@@ -14,8 +14,8 @@
 PIX = 48
 TL = 16
 SLOTS = 3
+NZ = 16
 LINE = SLOTS * TL
-NZ = 16
 F32 = jnp.float32
 BF16 = jnp.bfloat16
 MESH = pl.DeviceIdType.MESH
@@ -40,16 +40,14 @@
 ) = range(15)
 OPERANDS = 15
 STEM_LOADS = (PIXELS, STEM_WEIGHT, STEM_BIAS, REWARD, STEM_GAIN)
-OTHER_LOADS = (
-    TILE_COLS,
+EARLY_LOADS = (TILE_COLS, LATENT, UP_WEIGHT)
+LATE_LOADS = (
     TILE_COUNT,
-    LATENT,
-    UP_WEIGHT,
+    OUT_WEIGHT,
+    TAPS_TABLE,
     UP_BIAS,
     NORM_GAIN,
     NORM_BIAS,
-    OUT_WEIGHT,
-    TAPS_TABLE,
     LANES_TABLE,
 )
 TAPS = {(0, 0): (0,), (0, 1): (1, 2), (1, 0): (0, 1), (1, 1): (2,)}
@@ -73,14 +71,15 @@
 
 
 def cell_lanes():
-    table = np.zeros((128, 2, 2, 128), np.float32)
-    for c in range(3):
-        for dy in range(4):
-            for dx in range(4):
-                for copy in range(9):
-                    lane = copy * 12 + c * 4 + (dy % 2) * 2 + dx % 2
-                    table[c * 16 + dy * 4 + dx, dx // 2, dy // 2, lane] = 1
-    return table.reshape(128, 512)
+    table = np.zeros((2, 64, 2, 2, 2, 128), np.float32)
+    for odd in range(2):
+        for c in range(3):
+            for dy in range(4):
+                for dx in range(4):
+                    for copy in range(9):
+                        lane = copy * 12 + c * 4 + (dy % 2) * 2 + dx % 2
+                        table[odd, c * 16 + dy * 4 + dx, odd, dx // 2, dy // 2, lane] = 1
+    return table.reshape(128, 1024)
 
 
 def iota(shape, axis):
@@ -129,6 +128,7 @@
         margin_send,
         margin_recv,
         image,
+        x_send,
         x_recv,
         z_send,
         z_recv,
@@ -178,7 +178,7 @@
     def load(n):
         return pltpu.make_async_copy(operands[n], copies[n], load_sem.at[n])
 
-    for n in STEM_LOADS:
+    for n in STEM_LOADS + EARLY_LOADS:
         load(n).start()
 
     def greet_z(d, carry):
@@ -190,8 +190,6 @@
         greet(along_x(lax.rem(mx + d, nx)))
     greet(device(before))
     greet(device(after))
-    for n in OTHER_LOADS:
-        load(n).start()
 
     row_at = iota((CH, CH), 0)
     col_at = iota((CH, CH), 1)
@@ -202,9 +200,10 @@
     wide[0:LINE, :] = zeros[:, : 3 * CH]
     wide[17 * LINE : 18 * LINE, :] = zeros[:, : 3 * CH]
     out_rows[...] = jnp.zeros_like(out_rows)
-    reorder = (col_at == ((row_at >> 2) & 3) * (NZ * 4) + (row_at >> 4) * 4 + (row_at & 3)).astype(
-        F32
-    ).astype(BF16)
+    to_row = iota((128, 128), 0)
+    reorder = (
+        iota((128, 128), 1) == ((to_row >> 1) & 3) * (2 * NZ) + (to_row & 1) * NZ + (to_row >> 3)
+    ).astype(F32).astype(BF16)
     shift_low = ((col_at == row_at - 1) & ((row_at & 15) != 0)).astype(F32).astype(BF16)
     shift_high = ((col_at == row_at + 1) & ((row_at & 15) != 15)).astype(F32).astype(BF16)
     keep_before = block != 0
@@ -221,26 +220,28 @@
     stem = lax.dot_general(weight, pixels[...], TN, preferred_element_type=F32) + column_of(
         stem_bias[...]
     )
+    scaled = reward[...].astype(F32) * column_of(stem_gain[...])
     centred = stem - jnp.mean(stem, axis=0, keepdims=True)
+    scaled = scaled - jnp.mean(scaled, axis=0, keepdims=True)
     inverse = lax.rsqrt(jnp.mean(centred * centred, axis=0, keepdims=True) + EPS)
-    normed = centred * inverse
-    scaled = reward[...].astype(F32) * column_of(stem_gain[...])
-    stem_grad = (
-        scaled
-        - jnp.mean(scaled, axis=0, keepdims=True)
-        - normed * jnp.mean(scaled * normed, axis=0, keepdims=True)
-    ) * inverse
+    along = jnp.mean(scaled * centred, axis=0, keepdims=True) * inverse * inverse
+    stem_grad = (scaled - centred * along) * inverse
     padded_weight = jnp.concatenate([weight, jnp.zeros((128 - PIX, STEM), BF16)], axis=0)
     pixel_grad = dot(padded_weight, stem_grad.astype(BF16))
-    image[...] = pixel_grad.T.astype(BF16).reshape(nx, NZ * 4, 128)
-    x_recv[pl.ds(mx, 1)] = image[pl.ds(mx, 1)]
+    image[...] = pixel_grad.astype(BF16).astype(F32).T
+    left_half = iota((tiles, 128), 1) < 64
+    for h in range(2):
+        even, odd = [image[pl.ds(2 * h + n, tiles, stride=4), :] for n in range(2)]
+        both = jnp.where(left_half, even, pltpu.roll(odd, 64, 1)).astype(BF16)
+        x_send[:, h * NZ : (h + 1) * NZ, :] = both.reshape(nx, NZ, 128)
+    x_recv[pl.ds(mx, 1)] = x_send[pl.ds(mx, 1)]
 
     pl.semaphore_wait(barrier, 2 + (nx - 1) + (NZ - 1))
 
     def x_copy(d, slot):
         target = lax.rem(mx + d, nx)
         return pltpu.make_async_remote_copy(
-            src_ref=image.at[target],
+            src_ref=x_send.at[target],
             dst_ref=x_recv.at[slot],
             send_sem=xsend_sem.at[d - 1],
             recv_sem=xrecv_sem.at[d - 1],
@@ -250,19 +251,21 @@
 
     for d in range(1, nx):
         x_copy(d, mx).start()
+    for n in LATE_LOADS:
+        load(n).start()
 
     at3 = iota((SLOTS, blocks), 1)
     at1 = iota((1, blocks), 1)
-    for n in (TILE_COLS, TILE_COUNT, LATENT):
+    for n in (TILE_COLS, LATENT):
         load(n).wait()
     all_cols = tile_cols[...].astype(F32)
-    all_counts = tile_count[...].astype(F32)
 
     def columns(index):
         return jnp.sum(jnp.where(at3 == index, all_cols, 0.0), axis=1, keepdims=True)
 
     def count(index):
-        return jnp.sum(jnp.where(at1 == index, all_counts, 0.0), axis=1, keepdims=True)
+        counts = tile_count[...].astype(F32)
+        return jnp.sum(jnp.where(at1 == index, counts, 0.0), axis=1, keepdims=True)
 
     cols_own, cols_before, cols_after = columns(block), columns(before), columns(after)
 
@@ -312,7 +315,7 @@
                     at = (t * 2 + v) * CH
                     combined[r * 2 + s, at : at + CH, :] = total.astype(BF16)
 
-    for n in (UP_BIAS, NORM_GAIN, NORM_BIAS, OUT_WEIGHT, TAPS_TABLE, LANES_TABLE):
+    for n in (TILE_COUNT, UP_BIAS, NORM_GAIN, NORM_BIAS, OUT_WEIGHT, TAPS_TABLE, LANES_TABLE):
         load(n).wait()
     for ae in range(9):
         out_rows[ae * 8 : ae * 8 + 3, :] = out_weight[ae].astype(F32)
@@ -323,10 +326,9 @@
         ).astype(BF16)
 
     source = iota((1, 512), 1)
-    source_row = source & 3
-    source_x = (source >> 2) & 3
-    source_z = (source >> 4) & 15
-    cell_of = 2 * (source_x * NZ + source_z) + (source >> 8)
+    source_x, source_z = (source >> 1) & 3, (source >> 3) & 15
+    source_row = 2 * (source & 1) + (source >> 8)
+    cell_of = 2 * (source_x * NZ + source_z) + ((source >> 7) & 1)
     source_key = (cell_of + 1000 * source_row).astype(F32)
     own_rows = slot_rows(cols_own, 512)
     place_wide = (iota((LINE, 512), 0) & 15).astype(F32)
@@ -372,22 +374,22 @@
 
     for d in range(1, nx):
         x_copy(d, lax.rem(mx + nx - d, nx)).wait_recv()
-    by_z = dot(reorder, x_recv[...].reshape(nx * NZ * 4, 128)).astype(BF16)
-    z_send[...] = by_z.reshape(NZ, nx * 4, 128)
-
-    def z_copy(d, slot):
-        target = lax.rem(mz + d, NZ)
+    by_z = dot(reorder, x_recv[...].reshape(2 * tiles, 128))
+    z_send[...] = by_z.reshape(NZ, 2 * nx, 128).astype(BF16)
+
+    def z_copy(far, slot):
+        target = lax.rem(mz + far, NZ)
         return pltpu.make_async_remote_copy(
             src_ref=z_send.at[target],
             dst_ref=z_recv.at[slot],
-            send_sem=zsend_sem.at[d - 1],
-            recv_sem=zrecv_sem.at[d - 1],
+            send_sem=zsend_sem,
+            recv_sem=zrecv_sem,
             device_id=along_z(target),
             device_id_type=MESH,
         )
 
     def z_start(n, carry):
-        z_copy(1 + lax.rem(n + NZ // 2 - 1, NZ - 1), mz).start()
+        z_copy(NZ // 2 + (1 - 2 * lax.rem(n, 2)) * lax.div(n + 1, 2), mz).start()
         return carry
 
     lax.fori_loop(0, NZ - 1, z_start, 0)
@@ -479,13 +481,11 @@
 
     lax.fori_loop(0, 10, silu_slopes, 0)
 
-    def z_wait(d, carry):
-        z_copy(d, lax.rem(mz + NZ - d, NZ)).wait_recv()
-        return carry
-
-    lax.fori_loop(1, NZ, z_wait, 0)
-    spread = dot(z_recv[...].reshape(NZ * nx * 4, 128), lanes[...]).astype(BF16)
-    stacked = jnp.concatenate([spread[:, 0:256], spread[:, 256:512]], axis=0)
+    others = pl.ds(0, NZ - 1)
+    pltpu.make_async_copy(z_recv.at[others], z_recv.at[others], zrecv_sem).wait()
+    arrived = z_recv[...].astype(F32).reshape(2 * tiles, 128).astype(BF16)
+    spread = dot(arrived, lanes[...]).astype(BF16)
+    stacked = jnp.concatenate([spread[:, 256 * n : 256 * (n + 1)] for n in range(4)], axis=0)
     found = dot(choose, stacked)
     lane_wide = iota((1, 256), 1) & 127
     copy_wide = sum([(lane_wide >= 12 * c).astype(jnp.int32) for c in range(1, 9)])
@@ -606,12 +606,7 @@
     margin_copy(1, device(after)).wait_send()
     for d in range(1, nx):
         x_copy(d, mx).wait_send()
-
-    def z_sent(d, carry):
-        z_copy(d, mz).wait_send()
-        return carry
-
-    lax.fori_loop(1, NZ, z_sent, 0)
+    pltpu.make_async_copy(z_send.at[others], z_send.at[others], zsend_sem).wait()
     grad_copy(0, device(before)).wait_send()
     grad_copy(1, device(after)).wait_send()
 
@@ -665,10 +660,11 @@
             pltpu.VMEM((128, CH), F32),
             pltpu.VMEM((2, 4 * LINE, CH), BF16),
             pltpu.VMEM((2, 4 * LINE, CH), BF16),
-            pltpu.VMEM((nx, NZ * 4, 128), BF16),
-            pltpu.VMEM((nx, NZ * 4, 128), BF16),
-            pltpu.VMEM((NZ, nx * 4, 128), BF16),
-            pltpu.VMEM((NZ, nx * 4, 128), BF16),
+            pltpu.VMEM((4 * nx * NZ, 128), F32),
+            pltpu.VMEM((nx, 2 * NZ, 128), BF16),
+            pltpu.VMEM((nx, 2 * NZ, 128), BF16),
+            pltpu.VMEM((NZ, 2 * nx, 128), BF16),
+            pltpu.VMEM((NZ, 2 * nx, 128), BF16),
             pltpu.VMEM((4, TL * LINE, CH), F32),
             pltpu.VMEM((4, 10 * LINE, CH), F32),
             pltpu.VMEM((4, 10 * LINE, CH), F32),
@@ -683,8 +679,8 @@
             pltpu.SemaphoreType.DMA((2,)),
             pltpu.SemaphoreType.DMA((nx - 1,)),
             pltpu.SemaphoreType.DMA((nx - 1,)),
-            pltpu.SemaphoreType.DMA((NZ - 1,)),
-            pltpu.SemaphoreType.DMA((NZ - 1,)),
+            pltpu.SemaphoreType.DMA,
+            pltpu.SemaphoreType.DMA,
             pltpu.SemaphoreType.DMA((2,)),
             pltpu.SemaphoreType.DMA((2,)),
         ],

time: 36.5 us -> 36 us (0.986)
  Pallas kernels: 35.5 us -> 35 us
    pallas_call x1, Pallas kernels: 35.5 us -> 35 us  [per_device(): pl.pallas_call(functools.partial(kernel, nx, sections), out_shape=pltpu.V...]
where the time goes in v2:
time: 36 us; the launch traced here: 35.8 us
  Pallas kernels  35 us (97%)
  local copies, waits for them, and re-layouts  0.8 us (2%)
    pallas_call x1, Pallas kernels, per_device(): pl.pallas_call(functools.partial(kernel, nx, sections), out_shape=pltpu.V...  35 us
    unnamed x1, local copies, waits for them, and re-layouts  0.8 us

profile of v2, /device:TPU:1, one launch (start us, length us, event | category | flops | bytes accessed | tf_op | source)
XLA Modules:
  0.0 35.8 jit_solution(6343607524291564118)
XLA Ops:
  0.0 35.0 %shard_map.145 = bf16[8,128,256]{2,1,0:T(8,128)(2,1)S(1)} custom-call(bf16[8,128,256]{2,1,0:T(8,128)(2,1)} %refs_0_.1, bf16[192,256]{1,0:T(8,128)(2,1)} %bitcast.14, bf16[48,256]{1,0:T(8,128)(2,1)} %bitcast.15, bf16[3,3,256,256]{3,2,1,0:T(8,128)(2,1)} %refs_3_.1, f32[1,256]{1,0:T(1,128)} %bitcast.19, f32[1,256]{1,0:T(1,128)} %bitcast.20, f32[1,256]{1,0:T(1,128)} %bitcast.21, ...), custom_call_target="tpu_custom_call" | custom-call | tf_op jit(solution)/shard_map/pallas_call | solution.py:650
  35.0 0.8 %copy.17 = bf16[8,128,256]{2,1,0:T(8,128)(2,1)} copy(bf16[8,128,256]{2,1,0:T(8,128)(2,1)S(1)} %shard_map.145) | data formatting | bytes 1048576

commit v3 on v2

--- a/solution.py
+++ b/solution.py
@@ -50,7 +50,7 @@
     NORM_BIAS,
     LANES_TABLE,
 )
-TAPS = {(0, 0): (0,), (0, 1): (1, 2), (1, 0): (0, 1), (1, 1): (2,)}
+TAPS = ((0, 0), (0, 1), (1, 0), (1, 1))
 
 
 def out_taps():
@@ -181,11 +181,8 @@
     for n in STEM_LOADS + EARLY_LOADS:
         load(n).start()
 
-    def greet_z(d, carry):
+    for d in range(1, NZ):
         greet(along_z(lax.rem(mz + d, NZ)))
-        return carry
-
-    lax.fori_loop(1, NZ, greet_z, 0)
     for d in range(1, nx):
         greet(along_x(lax.rem(mx + d, nx)))
     greet(device(before))
@@ -251,9 +248,6 @@
 
     for d in range(1, nx):
         x_copy(d, mx).start()
-    for n in LATE_LOADS:
-        load(n).start()
-
     at3 = iota((SLOTS, blocks), 1)
     at1 = iota((1, blocks), 1)
     for n in (TILE_COLS, LATENT):
@@ -301,29 +295,8 @@
 
     margin_copy(0, device(before)).start()
     margin_copy(1, device(after)).start()
-
-    load(UP_WEIGHT).wait()
-    for r in range(2):
-        for s in range(2):
-            for t in range(2):
-                for v in range(2):
-                    total = None
-                    for a in TAPS[r, t]:
-                        for e in TAPS[s, v]:
-                            term = up_weight[a, e].astype(F32)
-                            total = term if total is None else total + term
-                    at = (t * 2 + v) * CH
-                    combined[r * 2 + s, at : at + CH, :] = total.astype(BF16)
-
-    for n in (TILE_COUNT, UP_BIAS, NORM_GAIN, NORM_BIAS, OUT_WEIGHT, TAPS_TABLE, LANES_TABLE):
-        load(n).wait()
-    for ae in range(9):
-        out_rows[ae * 8 : ae * 8 + 3, :] = out_weight[ae].astype(F32)
-    flat_taps = out_rows[...].astype(BF16)
-    for ph in range(4):
-        out_matrix[:, ph * CH : (ph + 1) * CH] = dot(
-            taps[ph * 128 : (ph + 1) * 128, :], flat_taps
-        ).astype(BF16)
+    for n in LATE_LOADS:
+        load(n).start()
 
     source = iota((1, 512), 1)
     source_x, source_z = (source >> 1) & 3, (source >> 3) & 15
@@ -343,6 +316,68 @@
         axis=0,
     )
 
+    for d in range(1, nx):
+        x_copy(d, lax.rem(mx + nx - d, nx)).wait_recv()
+    by_z = dot(reorder, x_recv[...].reshape(2 * tiles, 128))
+    z_send[...] = by_z.reshape(NZ, 2 * nx, 128).astype(BF16)
+
+    def z_copy(far, slot):
+        target = lax.rem(mz + far, NZ)
+        return pltpu.make_async_remote_copy(
+            src_ref=z_send.at[target],
+            dst_ref=z_recv.at[slot],
+            send_sem=zsend_sem,
+            recv_sem=zrecv_sem,
+            device_id=along_z(target),
+            device_id_type=MESH,
+        )
+
+    def z_start(n):
+        far = NZ // 2 + (1 - 2 * lax.rem(n, 2)) * lax.div(n + 1, 2)
+        target = lax.rem(mz + far, NZ)
+        pltpu.make_async_remote_copy(
+            src_ref=z_send.at[target],
+            dst_ref=z_recv.at[mz],
+            send_sem=zsend_sem,
+            recv_sem=zrecv_sem,
+            device_id=along_z(target),
+            device_id_type=MESH,
+        ).start()
+
+    def sums(first, second, third):
+        return {(0, 0): first, (0, 1): second + third, (1, 0): first + second, (1, 1): third}
+
+    def weight_rows(n):
+        rows = pl.ds(pl.multiple_of(n * 16, 16), 16)
+        by_col = []
+        for e in range(3):
+            by_col.append(sums(*[up_weight[a, e, rows, :].astype(F32) for a in range(3)]))
+        for r, t in TAPS:
+            by_tap = sums(*[by_col[e][r, t] for e in range(3)])
+            for s, v in TAPS:
+                at = pl.ds(pl.multiple_of((t * 2 + v) * CH + n * 16, 16), 16)
+                combined[r * 2 + s, at, :] = by_tap[s, v].astype(BF16)
+
+    def send_and_sum(n, carry):
+        z_start(n)
+        weight_rows(n)
+        return carry
+
+    load(UP_WEIGHT).wait()
+    lax.fori_loop(0, NZ - 1, send_and_sum, 0)
+    weight_rows(NZ - 1)
+    z_recv[pl.ds(mz, 1)] = z_send[pl.ds(mz, 1)]
+
+    for n in (TILE_COUNT, UP_BIAS, NORM_GAIN, NORM_BIAS, OUT_WEIGHT, TAPS_TABLE, LANES_TABLE):
+        load(n).wait()
+    for ae in range(9):
+        out_rows[ae * 8 : ae * 8 + 3, :] = out_weight[ae].astype(F32)
+    flat_taps = out_rows[...].astype(BF16)
+    for ph in range(4):
+        out_matrix[:, ph * CH : (ph + 1) * CH] = dot(
+            taps[ph * 128 : (ph + 1) * 128, :], flat_taps
+        ).astype(BF16)
+
     lane = iota((128, 128), 1)
     column = iota((128, 128), 0).astype(F32)
     slot_of = lane >> 4
@@ -371,29 +406,6 @@
     down_place = (
         own_place + place_columns(cols_after, jnp.where(keep_after, count(after), none), SLOTS)
     ).astype(BF16)
-
-    for d in range(1, nx):
-        x_copy(d, lax.rem(mx + nx - d, nx)).wait_recv()
-    by_z = dot(reorder, x_recv[...].reshape(2 * tiles, 128))
-    z_send[...] = by_z.reshape(NZ, 2 * nx, 128).astype(BF16)
-
-    def z_copy(far, slot):
-        target = lax.rem(mz + far, NZ)
-        return pltpu.make_async_remote_copy(
-            src_ref=z_send.at[target],
-            dst_ref=z_recv.at[slot],
-            send_sem=zsend_sem,
-            recv_sem=zrecv_sem,
-            device_id=along_z(target),
-            device_id_type=MESH,
-        )
-
-    def z_start(n, carry):
-        z_copy(NZ // 2 + (1 - 2 * lax.rem(n, 2)) * lax.div(n + 1, 2), mz).start()
-        return carry
-
-    lax.fori_loop(0, NZ - 1, z_start, 0)
-    z_recv[pl.ds(mz, 1)] = z_send[pl.ds(mz, 1)]
 
     margin_copy(0, device(before)).wait_recv()
     margin_copy(1, device(after)).wait_recv()
@@ -467,19 +479,23 @@
     inv = lax.rsqrt(variance + EPS)
     gain = jnp.broadcast_to(norm_gain[...], (LINE, CH))
     shift = jnp.broadcast_to(norm_bias[...], (LINE, CH))
-    inv_gain = inv * gain
+    half_gain = 0.5 * gain
+    half_scale = inv * half_gain
+    half_shift = 0.5 * shift
 
     def silu_slopes(n, carry):
-        for ph in range(4):
-            at = pl.ds(pl.multiple_of((n + 3) * LINE, LINE), LINE)
-            value = preact[ph, at, :] * inv_gain + shift
-            sigma = 0.5 * jnp.tanh(0.5 * value) + 0.5
-            slopes[ph, pl.ds(pl.multiple_of(n * LINE, LINE), LINE), :] = (
-                sigma * (1.0 + value * (1.0 - sigma)) * gain
-            )
+        for step in range(2):
+            source_at = pl.ds(pl.multiple_of((2 * n + step + 3) * LINE, LINE), LINE)
+            target_at = pl.ds(pl.multiple_of((2 * n + step) * LINE, LINE), LINE)
+            for ph in range(4):
+                half = preact[ph, source_at, :] * half_scale + half_shift
+                curve = jnp.tanh(half)
+                slopes[ph, target_at, :] = (
+                    (1.0 + curve) + half * (1.0 - curve * curve)
+                ) * half_gain
         return carry
 
-    lax.fori_loop(0, 10, silu_slopes, 0)
+    lax.fori_loop(0, 5, silu_slopes, 0)
 
     others = pl.ds(0, NZ - 1)
     pltpu.make_async_copy(z_recv.at[others], z_recv.at[others], zrecv_sem).wait()
@@ -565,50 +581,60 @@
             + jnp.where(place_rows > 0, pltpu.roll(parts[2], 1, 0), 0.0)
         ).astype(BF16)
 
-    def grad_copy(side, target):
+    def grad_copy(side, part):
+        rows = pl.ds((part if side == 0 else 1 - part) * 2 * LINE, 2 * LINE)
         return pltpu.make_async_remote_copy(
-            src_ref=grad_send.at[side],
-            dst_ref=grad_recv.at[1 - side],
-            send_sem=gsend_sem.at[side],
-            recv_sem=grecv_sem.at[1 - side],
-            device_id=target,
+            src_ref=grad_send.at[side, rows],
+            dst_ref=grad_recv.at[1 - side, rows],
+            send_sem=gsend_sem.at[side, part],
+            recv_sem=grecv_sem.at[1 - side, part],
+            device_id=device(after if side else before),
             device_id_type=MESH,
         )
 
-    for i in (0, 1, 2, 3, 4, 11, 12, 13, 14, 15):
+    for i in (0, 1, 2, 13, 14, 15):
         normal_grad(i)
-    margin_grad = input_grad(((0, 4), (12, 4)))
-    grad_send[0] = margin_grad[0 : 4 * LINE]
-    grad_send[1] = margin_grad[4 * LINE : 8 * LINE]
-    grad_copy(0, device(before)).start()
-    grad_copy(1, device(after)).start()
+    margin_grad = input_grad(((0, 2), (14, 2)))
+    grad_send[0, 0 : 2 * LINE, :] = margin_grad[0 : 2 * LINE]
+    grad_send[1, 2 * LINE : 4 * LINE, :] = margin_grad[2 * LINE : 4 * LINE]
+    grad_copy(0, 0).start()
+    grad_copy(1, 0).start()
+    for i in (3, 4, 11, 12):
+        normal_grad(i)
+    margin_grad = input_grad(((2, 2), (12, 2)))
+    grad_send[0, 2 * LINE : 4 * LINE, :] = margin_grad[0 : 2 * LINE]
+    grad_send[1, 0 : 2 * LINE, :] = margin_grad[2 * LINE : 4 * LINE]
+    grad_copy(0, 1).start()
+    grad_copy(1, 1).start()
     for i in range(5, 11):
         normal_grad(i)
     own_grad[...] = input_grad(((4, 8),))
 
-    grad_copy(0, device(before)).wait_recv()
-    grad_copy(1, device(after)).wait_recv()
     rest = jnp.zeros((128 - 2 * LINE, CH), BF16)
-    for r in range(8):
-        side = r // 4
-        at = (r % 4) * LINE
-        terms = jnp.concatenate(
-            [
-                own_grad[r * LINE : (r + 1) * LINE, :],
-                grad_recv[side, at : at + LINE, :],
-                rest,
-            ],
-            axis=0,
-        )
-        out[r] = dot(down_place if side else up_place, terms).astype(BF16)
+    for part, rows in ((0, (2, 3, 4, 5)), (1, (0, 1, 6, 7))):
+        grad_copy(0, part).wait_recv()
+        grad_copy(1, part).wait_recv()
+        for r in rows:
+            side = r // 4
+            at = (r % 4) * LINE
+            terms = jnp.concatenate(
+                [
+                    own_grad[r * LINE : (r + 1) * LINE, :],
+                    grad_recv[side, at : at + LINE, :],
+                    rest,
+                ],
+                axis=0,
+            )
+            out[r] = dot(down_place if side else up_place, terms).astype(BF16)
 
     margin_copy(0, device(before)).wait_send()
     margin_copy(1, device(after)).wait_send()
     for d in range(1, nx):
         x_copy(d, mx).wait_send()
     pltpu.make_async_copy(z_send.at[others], z_send.at[others], zsend_sem).wait()
-    grad_copy(0, device(before)).wait_send()
-    grad_copy(1, device(after)).wait_send()
+    for side in range(2):
+        for part in range(2):
+            grad_copy(side, part).wait_send()
 
 
 def per_device(
@@ -681,8 +707,8 @@
             pltpu.SemaphoreType.DMA((nx - 1,)),
             pltpu.SemaphoreType.DMA,
             pltpu.SemaphoreType.DMA,
-            pltpu.SemaphoreType.DMA((2,)),
-            pltpu.SemaphoreType.DMA((2,)),
+            pltpu.SemaphoreType.DMA((2, 2)),
+            pltpu.SemaphoreType.DMA((2, 2)),
         ],
         compiler_params=pltpu.CompilerParams(
             collective_id=0, has_side_effects=True, vmem_limit_bytes=48 * 1024 * 1024

time: 36 us -> 35.4 us (0.983)
  Pallas kernels: 35 us -> 34.5 us
    pallas_call x1, Pallas kernels: 35 us -> 34.5 us  [per_device(): pl.pallas_call(functools.partial(kernel, nx, sections), out_shape=pltpu.V...]
where the time goes in v3:
time: 35.4 us; the launch traced here: 35.3 us
  Pallas kernels  34.5 us (97%)
  local copies, waits for them, and re-layouts  0.8 us (2%)
    pallas_call x1, Pallas kernels, per_device(): pl.pallas_call(functools.partial(kernel, nx, sections), out_shape=pltpu.V...  34.5 us
    unnamed x1, local copies, waits for them, and re-layouts  0.8 us

profile of v3, /device:TPU:1, one launch (start us, length us, event | category | flops | bytes accessed | tf_op | source)
XLA Modules:
  0.0 35.3 jit_solution(6088959055966924133)
XLA Ops:
  0.0 34.5 %shard_map.145 = bf16[8,128,256]{2,1,0:T(8,128)(2,1)S(1)} custom-call(bf16[8,128,256]{2,1,0:T(8,128)(2,1)} %refs_0_.1, bf16[192,256]{1,0:T(8,128)(2,1)} %bitcast.14, bf16[48,256]{1,0:T(8,128)(2,1)} %bitcast.15, bf16[3,3,256,256]{3,2,1,0:T(8,128)(2,1)} %refs_3_.1, f32[1,256]{1,0:T(1,128)} %bitcast.19, f32[1,256]{1,0:T(1,128)} %bitcast.20, f32[1,256]{1,0:T(1,128)} %bitcast.21, ...), custom_call_target="tpu_custom_call" | custom-call | tf_op jit(solution)/shard_map/pallas_call | solution.py:676
  34.5 0.8 %copy.17 = bf16[8,128,256]{2,1,0:T(8,128)(2,1)} copy(bf16[8,128,256]{2,1,0:T(8,128)(2,1)S(1)} %shard_map.145) | data formatting | bytes 1048576

commit v4 on v3

--- a/solution.py
+++ b/solution.py
@@ -35,21 +35,13 @@
     STEM_GAIN,
     TILE_COUNT,
     TILE_COLS,
-    TAPS_TABLE,
-    LANES_TABLE,
-) = range(15)
-OPERANDS = 15
+    TABLES,
+) = range(14)
+OPERANDS = 14
 STEM_LOADS = (PIXELS, STEM_WEIGHT, STEM_BIAS, REWARD, STEM_GAIN)
-EARLY_LOADS = (TILE_COLS, LATENT, UP_WEIGHT)
-LATE_LOADS = (
-    TILE_COUNT,
-    OUT_WEIGHT,
-    TAPS_TABLE,
-    UP_BIAS,
-    NORM_GAIN,
-    NORM_BIAS,
-    LANES_TABLE,
-)
+BLOCK_LOADS = (TILE_COLS, TILE_COUNT)
+LARGE_LOADS = (LATENT, UP_WEIGHT)
+LATE_LOADS = (OUT_WEIGHT, TABLES, UP_BIAS, NORM_GAIN, NORM_BIAS)
 TAPS = ((0, 0), (0, 1), (1, 0), (1, 1))
 
 
@@ -67,7 +59,7 @@
                                 if 0 <= a < 3 and 0 <= e < 3:
                                     lane = (di * 3 + dj) * 12 + c * 4 + y * 2 + x
                                     table[r * 2 + s, lane, (a * 3 + e) * 8 + c] = 1
-    return table.reshape(512, 128)
+    return table.transpose(1, 0, 2).reshape(128, 512)
 
 
 def cell_lanes():
@@ -117,12 +109,12 @@
         stem_gain,
         tile_count,
         tile_cols,
-        taps,
-        lanes,
+        tables,
     ) = copies
     (
         wide,
         combined,
+        folded,
         out_matrix,
         out_rows,
         margin_send,
@@ -178,7 +170,7 @@
     def load(n):
         return pltpu.make_async_copy(operands[n], copies[n], load_sem.at[n])
 
-    for n in STEM_LOADS + EARLY_LOADS:
+    for n in BLOCK_LOADS + STEM_LOADS + LARGE_LOADS:
         load(n).start()
 
     for d in range(1, NZ):
@@ -191,11 +183,9 @@
     row_at = iota((CH, CH), 0)
     col_at = iota((CH, CH), 1)
     groups[...] = ((row_at >> 3) == (col_at >> 3)).astype(F32).astype(BF16)
-    zeros = jnp.zeros((LINE, 4 * CH), BF16)
-    zgrad[0:LINE, :] = zeros
-    zgrad[17 * LINE : 18 * LINE, :] = zeros
-    wide[0:LINE, :] = zeros[:, : 3 * CH]
-    wide[17 * LINE : 18 * LINE, :] = zeros[:, : 3 * CH]
+    zeros = jnp.zeros((LINE, 3 * CH), BF16)
+    wide[0:LINE, :] = zeros
+    wide[17 * LINE : 18 * LINE, :] = zeros
     out_rows[...] = jnp.zeros_like(out_rows)
     to_row = iota((128, 128), 0)
     reorder = (
@@ -205,6 +195,82 @@
     shift_high = ((col_at == row_at + 1) & ((row_at & 15) != 15)).astype(F32).astype(BF16)
     keep_before = block != 0
     keep_after = block != blocks - 1
+
+    at3 = iota((SLOTS, blocks), 1)
+    at1 = iota((1, blocks), 1)
+    for n in BLOCK_LOADS:
+        load(n).wait()
+    all_cols = tile_cols[...].astype(F32)
+
+    def columns(index):
+        return jnp.sum(jnp.where(at3 == index, all_cols, 0.0), axis=1, keepdims=True)
+
+    def count(index):
+        counts = tile_count[...].astype(F32)
+        return jnp.sum(jnp.where(at1 == index, counts, 0.0), axis=1, keepdims=True)
+
+    cols_own, cols_before, cols_after = columns(block), columns(before), columns(after)
+
+    def slot_rows(cols, width):
+        return jnp.concatenate(
+            [jnp.broadcast_to(cols[k : k + 1, :], (TL, width)) for k in range(SLOTS)], axis=0
+        )
+
+    place = (iota((LINE, 128), 0) & 15).astype(F32)
+    lane_f = iota((LINE, 128), 1).astype(F32)
+
+    def gather_rows(cols):
+        return (lane_f == slot_rows(cols, 128) + place).astype(F32)
+
+    pick_own = gather_rows(cols_own)
+    pick_up = jnp.concatenate([pick_own, gather_rows(cols_before)], axis=0).astype(BF16)
+    pick_down = jnp.concatenate([pick_own, gather_rows(cols_after)], axis=0).astype(BF16)
+    source = iota((1, 512), 1)
+    source_x, source_z = (source >> 1) & 3, (source >> 3) & 15
+    source_row = 2 * (source & 1) + (source >> 8)
+    cell_of = 2 * (source_x * NZ + source_z) + ((source >> 7) & 1)
+    source_key = (cell_of + 1000 * source_row).astype(F32)
+    own_rows = slot_rows(cols_own, 512)
+    place_wide = (iota((LINE, 512), 0) & 15).astype(F32)
+    inside = (place_wide >= 4.0) & (place_wide < 12.0)
+    choose = jnp.concatenate(
+        [
+            (jnp.where(inside, own_rows + place_wide + 1000.0 * pr, -1.0) == source_key)
+            .astype(F32)
+            .astype(BF16)
+            for pr in range(4)
+        ],
+        axis=0,
+    )
+
+    lane = iota((128, 128), 1)
+    column = iota((128, 128), 0).astype(F32)
+    slot_of = lane >> 4
+    offset_of = (lane & 15).astype(F32)
+
+    def place_columns(cols, live, first_slot):
+        start = jnp.where(
+            slot_of == first_slot,
+            jnp.broadcast_to(cols[0:1, :], (128, 128)),
+            jnp.where(
+                slot_of == first_slot + 1,
+                jnp.broadcast_to(cols[1:2, :], (128, 128)),
+                jnp.broadcast_to(cols[2:3, :], (128, 128)),
+            ),
+        )
+        relative = (slot_of - first_slot).astype(F32)
+        valid = (relative >= 0.0) & (relative < live) & (relative < float(SLOTS))
+        return jnp.where(valid & (column == start + offset_of), 1.0, 0.0)
+
+    none = jnp.zeros((1, 1), F32)
+    own_place = place_columns(cols_own, count(block), 0)
+    up_place = (
+        own_place
+        + place_columns(cols_before, jnp.where(keep_before, count(before), none), SLOTS)
+    ).astype(BF16)
+    down_place = (
+        own_place + place_columns(cols_after, jnp.where(keep_after, count(after), none), SLOTS)
+    ).astype(BF16)
 
     ones = jnp.ones((16, CH), BF16)
 
@@ -248,35 +314,7 @@
 
     for d in range(1, nx):
         x_copy(d, mx).start()
-    at3 = iota((SLOTS, blocks), 1)
-    at1 = iota((1, blocks), 1)
-    for n in (TILE_COLS, LATENT):
-        load(n).wait()
-    all_cols = tile_cols[...].astype(F32)
-
-    def columns(index):
-        return jnp.sum(jnp.where(at3 == index, all_cols, 0.0), axis=1, keepdims=True)
-
-    def count(index):
-        counts = tile_count[...].astype(F32)
-        return jnp.sum(jnp.where(at1 == index, counts, 0.0), axis=1, keepdims=True)
-
-    cols_own, cols_before, cols_after = columns(block), columns(before), columns(after)
-
-    def slot_rows(cols, width):
-        return jnp.concatenate(
-            [jnp.broadcast_to(cols[k : k + 1, :], (TL, width)) for k in range(SLOTS)], axis=0
-        )
-
-    place = (iota((LINE, 128), 0) & 15).astype(F32)
-    lane_f = iota((LINE, 128), 1).astype(F32)
-
-    def gather_rows(cols):
-        return (lane_f == slot_rows(cols, 128) + place).astype(F32)
-
-    pick_own = gather_rows(cols_own)
-    pick_up = jnp.concatenate([pick_own, gather_rows(cols_before)], axis=0).astype(BF16)
-    pick_down = jnp.concatenate([pick_own, gather_rows(cols_after)], axis=0).astype(BF16)
+    load(LATENT).wait()
     for r in range(8):
         side = r // 4
         rows = dot(pick_down if side else pick_up, latent[r]).astype(BF16)
@@ -297,24 +335,6 @@
     margin_copy(1, device(after)).start()
     for n in LATE_LOADS:
         load(n).start()
-
-    source = iota((1, 512), 1)
-    source_x, source_z = (source >> 1) & 3, (source >> 3) & 15
-    source_row = 2 * (source & 1) + (source >> 8)
-    cell_of = 2 * (source_x * NZ + source_z) + ((source >> 7) & 1)
-    source_key = (cell_of + 1000 * source_row).astype(F32)
-    own_rows = slot_rows(cols_own, 512)
-    place_wide = (iota((LINE, 512), 0) & 15).astype(F32)
-    inside = (place_wide >= 4.0) & (place_wide < 12.0)
-    choose = jnp.concatenate(
-        [
-            (jnp.where(inside, own_rows + place_wide + 1000.0 * pr, -1.0) == source_key)
-            .astype(F32)
-            .astype(BF16)
-            for pr in range(4)
-        ],
-        axis=0,
-    )
 
     for d in range(1, nx):
         x_copy(d, lax.rem(mx + nx - d, nx)).wait_recv()
@@ -349,14 +369,14 @@
 
     def weight_rows(n):
         rows = pl.ds(pl.multiple_of(n * 16, 16), 16)
-        by_col = []
-        for e in range(3):
-            by_col.append(sums(*[up_weight[a, e, rows, :].astype(F32) for a in range(3)]))
-        for r, t in TAPS:
-            by_tap = sums(*[by_col[e][r, t] for e in range(3)])
-            for s, v in TAPS:
+        by_col = [sums(*[up_weight[a, e, rows, :].astype(F32) for e in range(3)]) for a in range(3)]
+        for s, v in TAPS:
+            for a in range(3):
+                folded[a, s * 2 + v, rows, :] = by_col[a][s, v].astype(BF16)
+            by_tap = sums(*[by_col[a][s, v] for a in range(3)])
+            for r, t in TAPS:
                 at = pl.ds(pl.multiple_of((t * 2 + v) * CH + n * 16, 16), 16)
-                combined[r * 2 + s, at, :] = by_tap[s, v].astype(BF16)
+                combined[r * 2 + s, at, :] = by_tap[r, t].astype(BF16)
 
     def send_and_sum(n, carry):
         z_start(n)
@@ -368,44 +388,15 @@
     weight_rows(NZ - 1)
     z_recv[pl.ds(mz, 1)] = z_send[pl.ds(mz, 1)]
 
-    for n in (TILE_COUNT, UP_BIAS, NORM_GAIN, NORM_BIAS, OUT_WEIGHT, TAPS_TABLE, LANES_TABLE):
+    for n in LATE_LOADS:
         load(n).wait()
     for ae in range(9):
         out_rows[ae * 8 : ae * 8 + 3, :] = out_weight[ae].astype(F32)
     flat_taps = out_rows[...].astype(BF16)
     for ph in range(4):
         out_matrix[:, ph * CH : (ph + 1) * CH] = dot(
-            taps[ph * 128 : (ph + 1) * 128, :], flat_taps
+            tables[:, 1024 + ph * 128 : 1024 + (ph + 1) * 128], flat_taps
         ).astype(BF16)
-
-    lane = iota((128, 128), 1)
-    column = iota((128, 128), 0).astype(F32)
-    slot_of = lane >> 4
-    offset_of = (lane & 15).astype(F32)
-
-    def place_columns(cols, live, first_slot):
-        start = jnp.where(
-            slot_of == first_slot,
-            jnp.broadcast_to(cols[0:1, :], (128, 128)),
-            jnp.where(
-                slot_of == first_slot + 1,
-                jnp.broadcast_to(cols[1:2, :], (128, 128)),
-                jnp.broadcast_to(cols[2:3, :], (128, 128)),
-            ),
-        )
-        relative = (slot_of - first_slot).astype(F32)
-        valid = (relative >= 0.0) & (relative < live) & (relative < float(SLOTS))
-        return jnp.where(valid & (column == start + offset_of), 1.0, 0.0)
-
-    none = jnp.zeros((1, 1), F32)
-    own_place = place_columns(cols_own, count(block), 0)
-    up_place = (
-        own_place
-        + place_columns(cols_before, jnp.where(keep_before, count(before), none), SLOTS)
-    ).astype(BF16)
-    down_place = (
-        own_place + place_columns(cols_after, jnp.where(keep_after, count(after), none), SLOTS)
-    ).astype(BF16)
 
     margin_copy(0, device(before)).wait_recv()
     margin_copy(1, device(after)).wait_recv()
@@ -422,30 +413,16 @@
         wide[here, 2 * CH : 3 * CH] = dot(shift_high, inputs).astype(BF16)
 
     bias = up_bias[...]
-    total = jnp.zeros((LINE, CH), F32)
-    for ph in range(4):
-        r, s = ph // 2, ph % 2
-        features = jnp.concatenate(
-            [
-                wide[(r + t) * LINE : (r + t + TL) * LINE, s * CH : (s + 2) * CH]
-                for t in range(2)
-            ],
-            axis=1,
-        )
-        value = dot(features, combined[ph]) + bias
-        preact[ph] = value
-        total = total + jnp.sum(value.reshape(TL, LINE, CH), axis=0)
-
-    def group_means(sums):
+    def group_means(parts):
         rows = []
-        for term in sums:
+        for term in parts:
             high = term.astype(BF16).astype(F32)
             rest = term - high
             middle = rest.astype(BF16).astype(F32)
             rows += [high, middle, rest - middle]
         grouped = dot(jnp.concatenate(rows, axis=0).astype(BF16), groups[...])
         means = []
-        for n in range(len(sums)):
+        for n in range(len(parts)):
             first = grouped[3 * n * LINE : (3 * n + 1) * LINE]
             second = grouped[(3 * n + 1) * LINE : (3 * n + 2) * LINE]
             third = grouped[(3 * n + 2) * LINE : (3 * n + 3) * LINE]
@@ -463,25 +440,34 @@
             )
         return means
 
-    (mean,) = group_means([total])
-
-    def centre_rows(n, square):
-        for step in range(4):
-            at = pl.ds(pl.multiple_of((n * 4 + step) * LINE, LINE), LINE)
-            for ph in range(4):
-                off = preact[ph, at, :] - mean
-                preact[ph, at, :] = off
-                square = square + off * off
-        return square
-
-    square = lax.fori_loop(0, 4, centre_rows, jnp.zeros((LINE, CH), F32))
-    (variance,) = group_means([square])
-    inv = lax.rsqrt(variance + EPS)
+    def outputs(ph):
+        r, s = ph // 2, ph % 2
+        features = jnp.concatenate(
+            [
+                wide[(r + t) * LINE : (r + t + TL) * LINE, s * CH : (s + 2) * CH]
+                for t in range(2)
+            ],
+            axis=1,
+        )
+        return dot(features, combined[ph]).reshape(TL, LINE, CH)
+
+    value = outputs(0)
+    (centre,) = group_means([jnp.sum(value, axis=0) + bias * float(TL)])
+    to_centre = bias - 4.0 * centre
+    total = jnp.zeros((LINE, CH), F32)
+    square = jnp.zeros((LINE, CH), F32)
+    for ph in range(4):
+        off = (value if ph == 0 else outputs(ph)) + to_centre
+        preact[ph] = off.reshape(TL * LINE, CH)
+        total = total + jnp.sum(off, axis=0)
+        square = square + jnp.sum(off * off, axis=0)
+    mean, square = group_means([total, square])
+    inv = lax.rsqrt(jnp.maximum(square - mean * mean, 0.0) + EPS)
     gain = jnp.broadcast_to(norm_gain[...], (LINE, CH))
     shift = jnp.broadcast_to(norm_bias[...], (LINE, CH))
     half_gain = 0.5 * gain
     half_scale = inv * half_gain
-    half_shift = 0.5 * shift
+    half_shift = 0.5 * shift - mean * half_scale
 
     def silu_slopes(n, carry):
         for step in range(2):
@@ -500,7 +486,7 @@
     others = pl.ds(0, NZ - 1)
     pltpu.make_async_copy(z_recv.at[others], z_recv.at[others], zrecv_sem).wait()
     arrived = z_recv[...].astype(F32).reshape(2 * tiles, 128).astype(BF16)
-    spread = dot(arrived, lanes[...]).astype(BF16)
+    spread = dot(arrived, tables[:, 0:1024]).astype(BF16)
     stacked = jnp.concatenate([spread[:, 256 * n : 256 * (n + 1)] for n in range(4)], axis=0)
     found = dot(choose, stacked)
     lane_wide = iota((1, 256), 1) & 127
@@ -539,32 +525,47 @@
             second = second + grad * preact[ph, (n + 3) * LINE : (n + 4) * LINE, :]
     first, second = group_means([first, second])
     offset = first * inv
-    slope = second * inv * inv * inv
-
-    def normal_grad(i):
-        for ph in range(4):
-            value = -offset - preact[ph, i * LINE : (i + 1) * LINE, :] * slope
-            if 3 <= i < 13:
-                value = value + grads[ph, (i - 3) * LINE : (i - 2) * LINE, :] * inv
-            zgrad[(i + 1) * LINE : (i + 2) * LINE, ph * CH : (ph + 1) * CH] = value.astype(BF16)
+    slope = (second - mean * first) * inv * inv * inv
+    base = mean * slope - offset
+
+    def row_sums(evens, odds):
+        known = {}
+
+        def normal_grad(i, ph):
+            if (i, ph) not in known:
+                value = base - preact[ph, i * LINE : (i + 1) * LINE, :] * slope
+                if 3 <= i < 13:
+                    value = value + grads[ph, (i - 3) * LINE : (i - 2) * LINE, :] * inv
+                known[i, ph] = value
+            return known[i, ph]
+
+        for s in range(2):
+            lanes = slice(s * CH, (s + 1) * CH)
+            for i in sorted(set(evens) | set(odds)):
+                if i in evens:
+                    pair = normal_grad(i, s) + normal_grad(i, 2 + s)
+                    zgrad[0, i * LINE : (i + 1) * LINE, lanes] = pair.astype(BF16)
+                if i in odds:
+                    pair = [normal_grad(i, 2 + s)] if i >= 0 else []
+                    pair += [normal_grad(i + 1, s)] if i + 1 < TL else []
+                    zgrad[1, (i + 1) * LINE : (i + 2) * LINE, lanes] = sum(pair).astype(BF16)
 
     def input_grad(pieces):
         parts = []
         for pairs in (((0, 0),), ((0, 1), (1, 0)), ((1, 1),)):
             left, right = [], []
             for s, v in pairs:
-                for r in range(2):
-                    for t in range(2):
-                        ph = r * 2 + s
-                        rows = [
-                            zgrad[
-                                (i + 2 - r - t) * LINE : (i + 2 - r - t + lines_of) * LINE,
-                                ph * CH : (ph + 1) * CH,
-                            ]
-                            for i, lines_of in pieces
+                for a, kind, start in ((0, 1, 1), (1, 0, 0), (2, 1, 0)):
+                    rows = [
+                        zgrad[
+                            kind,
+                            (i + start) * LINE : (i + start + lines_of) * LINE,
+                            s * CH : (s + 1) * CH,
                         ]
-                        left.append(rows[0] if len(rows) == 1 else jnp.concatenate(rows, axis=0))
-                        right.append(combined[ph, (t * 2 + v) * CH : (t * 2 + v + 1) * CH, :])
+                        for i, lines_of in pieces
+                    ]
+                    left.append(rows[0] if len(rows) == 1 else jnp.concatenate(rows, axis=0))
+                    right.append(folded[a, s * 2 + v])
             parts.append(
                 lax.dot_general(
                     jnp.concatenate(left, axis=1),
@@ -592,22 +593,19 @@
             device_id_type=MESH,
         )
 
-    for i in (0, 1, 2, 13, 14, 15):
-        normal_grad(i)
+    row_sums((0, 1, 14, 15), (-1, 0, 1, 13, 14, 15))
     margin_grad = input_grad(((0, 2), (14, 2)))
     grad_send[0, 0 : 2 * LINE, :] = margin_grad[0 : 2 * LINE]
     grad_send[1, 2 * LINE : 4 * LINE, :] = margin_grad[2 * LINE : 4 * LINE]
     grad_copy(0, 0).start()
     grad_copy(1, 0).start()
-    for i in (3, 4, 11, 12):
-        normal_grad(i)
+    row_sums((2, 3, 12, 13), (2, 3, 11, 12))
     margin_grad = input_grad(((2, 2), (12, 2)))
     grad_send[0, 2 * LINE : 4 * LINE, :] = margin_grad[0 : 2 * LINE]
     grad_send[1, 0 : 2 * LINE, :] = margin_grad[2 * LINE : 4 * LINE]
     grad_copy(0, 1).start()
     grad_copy(1, 1).start()
-    for i in range(5, 11):
-        normal_grad(i)
+    row_sums(range(4, 12), range(4, 11))
     own_grad[...] = input_grad(((4, 8),))
 
     rest = jnp.zeros((128 - 2 * LINE, CH), BF16)
@@ -669,8 +667,7 @@
         stem_gain.reshape(1, STEM),
         tile_count.reshape(1, blocks),
         tile_cols.T,
-        jnp.asarray(out_taps(), BF16),
-        jnp.asarray(cell_lanes(), BF16),
+        jnp.asarray(np.concatenate([cell_lanes(), out_taps()], axis=1), BF16),
     )
     pinned = [pltpu.with_memory_space_constraint(array, pltpu.HBM) for array in operands]
     return pl.pallas_call(
@@ -682,6 +679,7 @@
         + [
             pltpu.VMEM((18 * LINE, 3 * CH), BF16),
             pltpu.VMEM((4, 4 * CH, CH), BF16),
+            pltpu.VMEM((3, 4, CH, CH), BF16),
             pltpu.VMEM((128, 4 * CH), BF16),
             pltpu.VMEM((128, CH), F32),
             pltpu.VMEM((2, 4 * LINE, CH), BF16),
@@ -694,7 +692,7 @@
             pltpu.VMEM((4, TL * LINE, CH), F32),
             pltpu.VMEM((4, 10 * LINE, CH), F32),
             pltpu.VMEM((4, 10 * LINE, CH), F32),
-            pltpu.VMEM((18 * LINE, 4 * CH), BF16),
+            pltpu.VMEM((2, 17 * LINE, 2 * CH), BF16),
             pltpu.VMEM((10 * LINE, 128), BF16),
             pltpu.VMEM((8 * LINE, CH), BF16),
             pltpu.VMEM((2, 4 * LINE, CH), BF16),

time: 35.4 us -> 35.2 us (level)
  no operation moved by 1% of the time
where the time goes in v4:
time: 35.2 us; the launch traced here: 35 us
  Pallas kernels  34.2 us (97%)
  local copies, waits for them, and re-layouts  0.8 us (2%)
    pallas_call x1, Pallas kernels, per_device(): pl.pallas_call(functools.partial(kernel, nx, sections), out_shape=pltpu.V...  34.2 us
    unnamed x1, local copies, waits for them, and re-layouts  0.8 us

profile of v4, /device:TPU:1, one launch (start us, length us, event | category | flops | bytes accessed | tf_op | source)
XLA Modules:
  0.0 35.0 jit_solution(9566466530151517282)
XLA Ops:
  0.0 34.2 %shard_map.136 = bf16[8,128,256]{2,1,0:T(8,128)(2,1)S(1)} custom-call(bf16[8,128,256]{2,1,0:T(8,128)(2,1)} %refs_0_.1, bf16[192,256]{1,0:T(8,128)(2,1)} %bitcast.14, bf16[48,256]{1,0:T(8,128)(2,1)} %bitcast.15, bf16[3,3,256,256]{3,2,1,0:T(8,128)(2,1)} %refs_3_.1, f32[1,256]{1,0:T(1,128)} %bitcast.19, f32[1,256]{1,0:T(1,128)} %bitcast.20, f32[1,256]{1,0:T(1,128)} %bitcast.21, ...), custom_call_target="tpu_custom_call" | custom-call | tf_op jit(solution)/shard_map/pallas_call | solution.py:673
  34.2 0.8 %copy.16 = bf16[8,128,256]{2,1,0:T(8,128)(2,1)} copy(bf16[8,128,256]{2,1,0:T(8,128)(2,1)S(1)} %shard_map.136) | data formatting | bytes 1048576

commit v5 on v4

--- a/solution.py
+++ b/solution.py
@@ -198,7 +198,7 @@
 
     at3 = iota((SLOTS, blocks), 1)
     at1 = iota((1, blocks), 1)
-    for n in BLOCK_LOADS:
+    for n in BLOCK_LOADS + STEM_LOADS + (LATENT,):
         load(n).wait()
     all_cols = tile_cols[...].astype(F32)
 
@@ -272,13 +272,18 @@
         own_place + place_columns(cols_after, jnp.where(keep_after, count(after), none), SLOTS)
     ).astype(BF16)
 
+    for r in range(8):
+        side = r // 4
+        rows = dot(pick_down if side else pick_up, latent[r]).astype(BF16)
+        wide[(5 + r) * LINE : (6 + r) * LINE, CH : 2 * CH] = rows[0:LINE]
+        margin_send[side, (r % 4) * LINE : (r % 4 + 1) * LINE, :] = rows[LINE : 2 * LINE]
+
+
     ones = jnp.ones((16, CH), BF16)
 
     def column_of(row):
         return lax.dot_general(three_rows(row), ones, TN, preferred_element_type=F32)
 
-    for n in STEM_LOADS:
-        load(n).wait()
     weight = stem_weight[...]
     stem = lax.dot_general(weight, pixels[...], TN, preferred_element_type=F32) + column_of(
         stem_bias[...]
@@ -301,6 +306,19 @@
 
     pl.semaphore_wait(barrier, 2 + (nx - 1) + (NZ - 1))
 
+    def margin_copy(side, target):
+        return pltpu.make_async_remote_copy(
+            src_ref=margin_send.at[side],
+            dst_ref=margin_recv.at[1 - side],
+            send_sem=msend_sem.at[side],
+            recv_sem=mrecv_sem.at[1 - side],
+            device_id=target,
+            device_id_type=MESH,
+        )
+
+    margin_copy(0, device(before)).start()
+    margin_copy(1, device(after)).start()
+
     def x_copy(d, slot):
         target = lax.rem(mx + d, nx)
         return pltpu.make_async_remote_copy(
@@ -314,43 +332,43 @@
 
     for d in range(1, nx):
         x_copy(d, mx).start()
-    load(LATENT).wait()
-    for r in range(8):
-        side = r // 4
-        rows = dot(pick_down if side else pick_up, latent[r]).astype(BF16)
-        wide[(5 + r) * LINE : (6 + r) * LINE, CH : 2 * CH] = rows[0:LINE]
-        margin_send[side, (r % 4) * LINE : (r % 4 + 1) * LINE, :] = rows[LINE : 2 * LINE]
-
-    def margin_copy(side, target):
-        return pltpu.make_async_remote_copy(
-            src_ref=margin_send.at[side],
-            dst_ref=margin_recv.at[1 - side],
-            send_sem=msend_sem.at[side],
-            recv_sem=mrecv_sem.at[1 - side],
-            device_id=target,
-            device_id_type=MESH,
-        )
-
-    margin_copy(0, device(before)).start()
-    margin_copy(1, device(after)).start()
     for n in LATE_LOADS:
         load(n).start()
+
+    def sums(first, second, third):
+        return {(0, 0): first, (0, 1): second + third, (1, 0): first + second, (1, 1): third}
+
+    def weight_rows(n):
+        rows = pl.ds(pl.multiple_of(n * 16, 16), 16)
+        by_col = [sums(*[up_weight[a, e, rows, :].astype(F32) for e in range(3)]) for a in range(3)]
+        for s, v in TAPS:
+            for a in range(3):
+                folded[a, s * 2 + v, rows, :] = by_col[a][s, v].astype(BF16)
+            by_tap = sums(*[by_col[a][s, v] for a in range(3)])
+            for r, t in TAPS:
+                at = pl.ds(pl.multiple_of((t * 2 + v) * CH + n * 16, 16), 16)
+                combined[r * 2 + s, at, :] = by_tap[r, t].astype(BF16)
+
+    def weight_chunk(n, carry):
+        weight_rows(n)
+        return carry
+
+    load(UP_WEIGHT).wait()
+    lax.fori_loop(0, CH // 16, weight_chunk, 0)
+    for n in LATE_LOADS:
+        load(n).wait()
+    for ae in range(9):
+        out_rows[ae * 8 : ae * 8 + 3, :] = out_weight[ae].astype(F32)
+    flat_taps = out_rows[...].astype(BF16)
+    for ph in range(4):
+        out_matrix[:, ph * CH : (ph + 1) * CH] = dot(
+            tables[:, 1024 + ph * 128 : 1024 + (ph + 1) * 128], flat_taps
+        ).astype(BF16)
 
     for d in range(1, nx):
         x_copy(d, lax.rem(mx + nx - d, nx)).wait_recv()
     by_z = dot(reorder, x_recv[...].reshape(2 * tiles, 128))
     z_send[...] = by_z.reshape(NZ, 2 * nx, 128).astype(BF16)
-
-    def z_copy(far, slot):
-        target = lax.rem(mz + far, NZ)
-        return pltpu.make_async_remote_copy(
-            src_ref=z_send.at[target],
-            dst_ref=z_recv.at[slot],
-            send_sem=zsend_sem,
-            recv_sem=zrecv_sem,
-            device_id=along_z(target),
-            device_id_type=MESH,
-        )
 
     def z_start(n):
         far = NZ // 2 + (1 - 2 * lax.rem(n, 2)) * lax.div(n + 1, 2)
@@ -364,39 +382,12 @@
             device_id_type=MESH,
         ).start()
 
-    def sums(first, second, third):
-        return {(0, 0): first, (0, 1): second + third, (1, 0): first + second, (1, 1): third}
-
-    def weight_rows(n):
-        rows = pl.ds(pl.multiple_of(n * 16, 16), 16)
-        by_col = [sums(*[up_weight[a, e, rows, :].astype(F32) for e in range(3)]) for a in range(3)]
-        for s, v in TAPS:
-            for a in range(3):
-                folded[a, s * 2 + v, rows, :] = by_col[a][s, v].astype(BF16)
-            by_tap = sums(*[by_col[a][s, v] for a in range(3)])
-            for r, t in TAPS:
-                at = pl.ds(pl.multiple_of((t * 2 + v) * CH + n * 16, 16), 16)
-                combined[r * 2 + s, at, :] = by_tap[r, t].astype(BF16)
-
-    def send_and_sum(n, carry):
+    def z_send_one(n, carry):
         z_start(n)
-        weight_rows(n)
         return carry
 
-    load(UP_WEIGHT).wait()
-    lax.fori_loop(0, NZ - 1, send_and_sum, 0)
-    weight_rows(NZ - 1)
+    lax.fori_loop(0, NZ - 1, z_send_one, 0)
     z_recv[pl.ds(mz, 1)] = z_send[pl.ds(mz, 1)]
-
-    for n in LATE_LOADS:
-        load(n).wait()
-    for ae in range(9):
-        out_rows[ae * 8 : ae * 8 + 3, :] = out_weight[ae].astype(F32)
-    flat_taps = out_rows[...].astype(BF16)
-    for ph in range(4):
-        out_matrix[:, ph * CH : (ph + 1) * CH] = dot(
-            tables[:, 1024 + ph * 128 : 1024 + (ph + 1) * 128], flat_taps
-        ).astype(BF16)
 
     margin_copy(0, device(before)).wait_recv()
     margin_copy(1, device(after)).wait_recv()

time: 35.2 us -> 35 us (level)
  no operation moved by 1% of the time
where the time goes in v5:
time: 35 us; the launch traced here: 34.9 us
  Pallas kernels  34.1 us (97%)
  local copies, waits for them, and re-layouts  0.8 us (2%)
    pallas_call x1, Pallas kernels, per_device(): pl.pallas_call(functools.partial(kernel, nx, sections), out_shape=pltpu.V...  34.1 us
    unnamed x1, local copies, waits for them, and re-layouts  0.8 us

profile of v5, /device:TPU:1, one launch (start us, length us, event | category | flops | bytes accessed | tf_op | source)
XLA Modules:
  0.0 34.9 jit_solution(2375354896998132427)
XLA Ops:
  0.0 34.1 %shard_map.136 = bf16[8,128,256]{2,1,0:T(8,128)(2,1)S(1)} custom-call(bf16[8,128,256]{2,1,0:T(8,128)(2,1)} %refs_0_.1, bf16[192,256]{1,0:T(8,128)(2,1)} %bitcast.14, bf16[48,256]{1,0:T(8,128)(2,1)} %bitcast.15, bf16[3,3,256,256]{3,2,1,0:T(8,128)(2,1)} %refs_3_.1, f32[1,256]{1,0:T(1,128)} %bitcast.19, f32[1,256]{1,0:T(1,128)} %bitcast.20, f32[1,256]{1,0:T(1,128)} %bitcast.21, ...), custom_call_target="tpu_custom_call" | custom-call | tf_op jit(solution)/shard_map/pallas_call | solution.py:664
  34.1 0.8 %copy.16 = bf16[8,128,256]{2,1,0:T(8,128)(2,1)} copy(bf16[8,128,256]{2,1,0:T(8,128)(2,1)S(1)} %shard_map.136) | data formatting | bytes 1048576

commit v6 on v5

--- a/solution.py
+++ b/solution.py
@@ -40,7 +40,6 @@
 OPERANDS = 14
 STEM_LOADS = (PIXELS, STEM_WEIGHT, STEM_BIAS, REWARD, STEM_GAIN)
 BLOCK_LOADS = (TILE_COLS, TILE_COUNT)
-LARGE_LOADS = (LATENT, UP_WEIGHT)
 LATE_LOADS = (OUT_WEIGHT, TABLES, UP_BIAS, NORM_GAIN, NORM_BIAS)
 TAPS = ((0, 0), (0, 1), (1, 0), (1, 1))
 
@@ -170,7 +169,7 @@
     def load(n):
         return pltpu.make_async_copy(operands[n], copies[n], load_sem.at[n])
 
-    for n in BLOCK_LOADS + STEM_LOADS + LARGE_LOADS:
+    for n in BLOCK_LOADS + (LATENT,) + STEM_LOADS + (UP_WEIGHT,):
         load(n).start()
 
     for d in range(1, NZ):
@@ -198,7 +197,7 @@
 
     at3 = iota((SLOTS, blocks), 1)
     at1 = iota((1, blocks), 1)
-    for n in BLOCK_LOADS + STEM_LOADS + (LATENT,):
+    for n in BLOCK_LOADS + (LATENT,):
         load(n).wait()
     all_cols = tile_cols[...].astype(F32)
 
@@ -225,53 +224,6 @@
     pick_own = gather_rows(cols_own)
     pick_up = jnp.concatenate([pick_own, gather_rows(cols_before)], axis=0).astype(BF16)
     pick_down = jnp.concatenate([pick_own, gather_rows(cols_after)], axis=0).astype(BF16)
-    source = iota((1, 512), 1)
-    source_x, source_z = (source >> 1) & 3, (source >> 3) & 15
-    source_row = 2 * (source & 1) + (source >> 8)
-    cell_of = 2 * (source_x * NZ + source_z) + ((source >> 7) & 1)
-    source_key = (cell_of + 1000 * source_row).astype(F32)
-    own_rows = slot_rows(cols_own, 512)
-    place_wide = (iota((LINE, 512), 0) & 15).astype(F32)
-    inside = (place_wide >= 4.0) & (place_wide < 12.0)
-    choose = jnp.concatenate(
-        [
-            (jnp.where(inside, own_rows + place_wide + 1000.0 * pr, -1.0) == source_key)
-            .astype(F32)
-            .astype(BF16)
-            for pr in range(4)
-        ],
-        axis=0,
-    )
-
-    lane = iota((128, 128), 1)
-    column = iota((128, 128), 0).astype(F32)
-    slot_of = lane >> 4
-    offset_of = (lane & 15).astype(F32)
-
-    def place_columns(cols, live, first_slot):
-        start = jnp.where(
-            slot_of == first_slot,
-            jnp.broadcast_to(cols[0:1, :], (128, 128)),
-            jnp.where(
-                slot_of == first_slot + 1,
-                jnp.broadcast_to(cols[1:2, :], (128, 128)),
-                jnp.broadcast_to(cols[2:3, :], (128, 128)),
-            ),
-        )
-        relative = (slot_of - first_slot).astype(F32)
-        valid = (relative >= 0.0) & (relative < live) & (relative < float(SLOTS))
-        return jnp.where(valid & (column == start + offset_of), 1.0, 0.0)
-
-    none = jnp.zeros((1, 1), F32)
-    own_place = place_columns(cols_own, count(block), 0)
-    up_place = (
-        own_place
-        + place_columns(cols_before, jnp.where(keep_before, count(before), none), SLOTS)
-    ).astype(BF16)
-    down_place = (
-        own_place + place_columns(cols_after, jnp.where(keep_after, count(after), none), SLOTS)
-    ).astype(BF16)
-
     for r in range(8):
         side = r // 4
         rows = dot(pick_down if side else pick_up, latent[r]).astype(BF16)
@@ -279,11 +231,28 @@
         margin_send[side, (r % 4) * LINE : (r % 4 + 1) * LINE, :] = rows[LINE : 2 * LINE]
 
 
+    pl.semaphore_wait(barrier, 2 + (nx - 1) + (NZ - 1))
+
+    def margin_copy(side, target):
+        return pltpu.make_async_remote_copy(
+            src_ref=margin_send.at[side],
+            dst_ref=margin_recv.at[1 - side],
+            send_sem=msend_sem.at[side],
+            recv_sem=mrecv_sem.at[1 - side],
+            device_id=target,
+            device_id_type=MESH,
+        )
+
+    margin_copy(0, device(before)).start()
+    margin_copy(1, device(after)).start()
+
     ones = jnp.ones((16, CH), BF16)
 
     def column_of(row):
         return lax.dot_general(three_rows(row), ones, TN, preferred_element_type=F32)
 
+    for n in STEM_LOADS:
+        load(n).wait()
     weight = stem_weight[...]
     stem = lax.dot_general(weight, pixels[...], TN, preferred_element_type=F32) + column_of(
         stem_bias[...]
@@ -304,21 +273,6 @@
         x_send[:, h * NZ : (h + 1) * NZ, :] = both.reshape(nx, NZ, 128)
     x_recv[pl.ds(mx, 1)] = x_send[pl.ds(mx, 1)]
 
-    pl.semaphore_wait(barrier, 2 + (nx - 1) + (NZ - 1))
-
-    def margin_copy(side, target):
-        return pltpu.make_async_remote_copy(
-            src_ref=margin_send.at[side],
-            dst_ref=margin_recv.at[1 - side],
-            send_sem=msend_sem.at[side],
-            recv_sem=mrecv_sem.at[1 - side],
-            device_id=target,
-            device_id_type=MESH,
-        )
-
-    margin_copy(0, device(before)).start()
-    margin_copy(1, device(after)).start()
-
     def x_copy(d, slot):
         target = lax.rem(mx + d, nx)
         return pltpu.make_async_remote_copy(
@@ -334,6 +288,53 @@
         x_copy(d, mx).start()
     for n in LATE_LOADS:
         load(n).start()
+
+    source = iota((1, 512), 1)
+    source_x, source_z = (source >> 1) & 3, (source >> 3) & 15
+    source_row = 2 * (source & 1) + (source >> 8)
+    cell_of = 2 * (source_x * NZ + source_z) + ((source >> 7) & 1)
+    source_key = (cell_of + 1000 * source_row).astype(F32)
+    own_rows = slot_rows(cols_own, 512)
+    place_wide = (iota((LINE, 512), 0) & 15).astype(F32)
+    inside = (place_wide >= 4.0) & (place_wide < 12.0)
+    choose = jnp.concatenate(
+        [
+            (jnp.where(inside, own_rows + place_wide + 1000.0 * pr, -1.0) == source_key)
+            .astype(F32)
+            .astype(BF16)
+            for pr in range(4)
+        ],
+        axis=0,
+    )
+
+    lane = iota((128, 128), 1)
+    column = iota((128, 128), 0).astype(F32)
+    slot_of = lane >> 4
+    offset_of = (lane & 15).astype(F32)
+
+    def place_columns(cols, live, first_slot):
+        start = jnp.where(
+            slot_of == first_slot,
+            jnp.broadcast_to(cols[0:1, :], (128, 128)),
+            jnp.where(
+                slot_of == first_slot + 1,
+                jnp.broadcast_to(cols[1:2, :], (128, 128)),
+                jnp.broadcast_to(cols[2:3, :], (128, 128)),
+            ),
+        )
+        relative = (slot_of - first_slot).astype(F32)
+        valid = (relative >= 0.0) & (relative < live) & (relative < float(SLOTS))
+        return jnp.where(valid & (column == start + offset_of), 1.0, 0.0)
+
+    none = jnp.zeros((1, 1), F32)
+    own_place = place_columns(cols_own, count(block), 0)
+    up_place = (
+        own_place
+        + place_columns(cols_before, jnp.where(keep_before, count(before), none), SLOTS)
+    ).astype(BF16)
+    down_place = (
+        own_place + place_columns(cols_after, jnp.where(keep_after, count(after), none), SLOTS)
+    ).astype(BF16)
 
     def sums(first, second, third):
         return {(0, 0): first, (0, 1): second + third, (1, 0): first + second, (1, 1): third}

time: 35 us -> 35.7 us (1.020)
  Pallas kernels: 34.1 us -> 34.8 us
    pallas_call x1, Pallas kernels: 34.1 us -> 34.8 us  [per_device(): pl.pallas_call(functools.partial(kernel, nx, sections), out_shape=pltpu.V...]
where the time goes in v6:
time: 35.7 us; the launch traced here: 35.6 us
  Pallas kernels  34.8 us (97%)
  local copies, waits for them, and re-layouts  0.8 us (2%)
    pallas_call x1, Pallas kernels, per_device(): pl.pallas_call(functools.partial(kernel, nx, sections), out_shape=pltpu.V...  34.8 us
    unnamed x1, local copies, waits for them, and re-layouts  0.8 us

profile of v6, /device:TPU:1, one launch (start us, length us, event | category | flops | bytes accessed | tf_op | source)
XLA Modules:
  0.0 35.6 jit_solution(5775463732766045436)
XLA Ops:
  0.0 34.8 %shard_map.136 = bf16[8,128,256]{2,1,0:T(8,128)(2,1)S(1)} custom-call(bf16[8,128,256]{2,1,0:T(8,128)(2,1)} %refs_0_.1, bf16[192,256]{1,0:T(8,128)(2,1)} %bitcast.14, bf16[48,256]{1,0:T(8,128)(2,1)} %bitcast.15, bf16[3,3,256,256]{3,2,1,0:T(8,128)(2,1)} %refs_3_.1, f32[1,256]{1,0:T(1,128)} %bitcast.19, f32[1,256]{1,0:T(1,128)} %bitcast.20, f32[1,256]{1,0:T(1,128)} %bitcast.21, ...), custom_call_target="tpu_custom_call" | custom-call | tf_op jit(solution)/shard_map/pallas_call | solution.py:665
  34.8 0.8 %copy.16 = bf16[8,128,256]{2,1,0:T(8,128)(2,1)} copy(bf16[8,128,256]{2,1,0:T(8,128)(2,1)S(1)} %shard_map.136) | data formatting | bytes 1048576

commit v7 on v6

--- a/solution.py
+++ b/solution.py
@@ -40,6 +40,7 @@
 OPERANDS = 14
 STEM_LOADS = (PIXELS, STEM_WEIGHT, STEM_BIAS, REWARD, STEM_GAIN)
 BLOCK_LOADS = (TILE_COLS, TILE_COUNT)
+LARGE_LOADS = (LATENT, UP_WEIGHT)
 LATE_LOADS = (OUT_WEIGHT, TABLES, UP_BIAS, NORM_GAIN, NORM_BIAS)
 TAPS = ((0, 0), (0, 1), (1, 0), (1, 1))
 
@@ -169,7 +170,7 @@
     def load(n):
         return pltpu.make_async_copy(operands[n], copies[n], load_sem.at[n])
 
-    for n in BLOCK_LOADS + (LATENT,) + STEM_LOADS + (UP_WEIGHT,):
+    for n in BLOCK_LOADS + STEM_LOADS + LARGE_LOADS:
         load(n).start()
 
     for d in range(1, NZ):
@@ -197,7 +198,7 @@
 
     at3 = iota((SLOTS, blocks), 1)
     at1 = iota((1, blocks), 1)
-    for n in BLOCK_LOADS + (LATENT,):
+    for n in BLOCK_LOADS + STEM_LOADS + (LATENT,):
         load(n).wait()
     all_cols = tile_cols[...].astype(F32)
 
@@ -231,28 +232,11 @@
         margin_send[side, (r % 4) * LINE : (r % 4 + 1) * LINE, :] = rows[LINE : 2 * LINE]
 
 
-    pl.semaphore_wait(barrier, 2 + (nx - 1) + (NZ - 1))
-
-    def margin_copy(side, target):
-        return pltpu.make_async_remote_copy(
-            src_ref=margin_send.at[side],
-            dst_ref=margin_recv.at[1 - side],
-            send_sem=msend_sem.at[side],
-            recv_sem=mrecv_sem.at[1 - side],
-            device_id=target,
-            device_id_type=MESH,
-        )
-
-    margin_copy(0, device(before)).start()
-    margin_copy(1, device(after)).start()
-
     ones = jnp.ones((16, CH), BF16)
 
     def column_of(row):
         return lax.dot_general(three_rows(row), ones, TN, preferred_element_type=F32)
 
-    for n in STEM_LOADS:
-        load(n).wait()
     weight = stem_weight[...]
     stem = lax.dot_general(weight, pixels[...], TN, preferred_element_type=F32) + column_of(
         stem_bias[...]
@@ -273,6 +257,21 @@
         x_send[:, h * NZ : (h + 1) * NZ, :] = both.reshape(nx, NZ, 128)
     x_recv[pl.ds(mx, 1)] = x_send[pl.ds(mx, 1)]
 
+    pl.semaphore_wait(barrier, 2 + (nx - 1) + (NZ - 1))
+
+    def margin_copy(side, target):
+        return pltpu.make_async_remote_copy(
+            src_ref=margin_send.at[side],
+            dst_ref=margin_recv.at[1 - side],
+            send_sem=msend_sem.at[side],
+            recv_sem=mrecv_sem.at[1 - side],
+            device_id=target,
+            device_id_type=MESH,
+        )
+
+    margin_copy(0, device(before)).start()
+    margin_copy(1, device(after)).start()
+
     def x_copy(d, slot):
         target = lax.rem(mx + d, nx)
         return pltpu.make_async_remote_copy(
@@ -289,6 +288,26 @@
     for n in LATE_LOADS:
         load(n).start()
 
+    def sums(first, second, third):
+        return {(0, 0): first, (0, 1): second + third, (1, 0): first + second, (1, 1): third}
+
+    def weight_rows(n):
+        rows = pl.ds(pl.multiple_of(n * 16, 16), 16)
+        by_col = [sums(*[up_weight[a, e, rows, :].astype(F32) for e in range(3)]) for a in range(3)]
+        for s, v in TAPS:
+            for a in range(3):
+                folded[a, s * 2 + v, rows, :] = by_col[a][s, v].astype(BF16)
+            by_tap = sums(*[by_col[a][s, v] for a in range(3)])
+            for r, t in TAPS:
+                at = pl.ds(pl.multiple_of((t * 2 + v) * CH + n * 16, 16), 16)
+                combined[r * 2 + s, at, :] = by_tap[r, t].astype(BF16)
+
+    def weight_chunk(n, carry):
+        weight_rows(n)
+        return carry
+
+    load(UP_WEIGHT).wait()
+    lax.fori_loop(0, CH // 16, weight_chunk, 0)
     source = iota((1, 512), 1)
     source_x, source_z = (source >> 1) & 3, (source >> 3) & 15
     source_row = 2 * (source & 1) + (source >> 8)
@@ -336,26 +355,6 @@
         own_place + place_columns(cols_after, jnp.where(keep_after, count(after), none), SLOTS)
     ).astype(BF16)
 
-    def sums(first, second, third):
-        return {(0, 0): first, (0, 1): second + third, (1, 0): first + second, (1, 1): third}
-
-    def weight_rows(n):
-        rows = pl.ds(pl.multiple_of(n * 16, 16), 16)
-        by_col = [sums(*[up_weight[a, e, rows, :].astype(F32) for e in range(3)]) for a in range(3)]
-        for s, v in TAPS:
-            for a in range(3):
-                folded[a, s * 2 + v, rows, :] = by_col[a][s, v].astype(BF16)
-            by_tap = sums(*[by_col[a][s, v] for a in range(3)])
-            for r, t in TAPS:
-                at = pl.ds(pl.multiple_of((t * 2 + v) * CH + n * 16, 16), 16)
-                combined[r * 2 + s, at, :] = by_tap[r, t].astype(BF16)
-
-    def weight_chunk(n, carry):
-        weight_rows(n)
-        return carry
-
-    load(UP_WEIGHT).wait()
-    lax.fori_loop(0, CH // 16, weight_chunk, 0)
     for n in LATE_LOADS:
         load(n).wait()
     for ae in range(9):
@@ -371,8 +370,7 @@
     by_z = dot(reorder, x_recv[...].reshape(2 * tiles, 128))
     z_send[...] = by_z.reshape(NZ, 2 * nx, 128).astype(BF16)
 
-    def z_start(n):
-        far = NZ // 2 + (1 - 2 * lax.rem(n, 2)) * lax.div(n + 1, 2)
+    for far in (8, 7, 9, 6, 10, 5, 11, 4, 12, 3, 13, 2, 14, 1, 15):
         target = lax.rem(mz + far, NZ)
         pltpu.make_async_remote_copy(
             src_ref=z_send.at[target],
@@ -382,12 +380,6 @@
             device_id=along_z(target),
             device_id_type=MESH,
         ).start()
-
-    def z_send_one(n, carry):
-        z_start(n)
-        return carry
-
-    lax.fori_loop(0, NZ - 1, z_send_one, 0)
     z_recv[pl.ds(mz, 1)] = z_send[pl.ds(mz, 1)]
 
     margin_copy(0, device(before)).wait_recv()
@@ -600,6 +592,12 @@
     row_sums(range(4, 12), range(4, 11))
     own_grad[...] = input_grad(((4, 8),))
 
+    margin_copy(0, device(before)).wait_send()
+    margin_copy(1, device(after)).wait_send()
+    for d in range(1, nx):
+        x_copy(d, mx).wait_send()
+    pltpu.make_async_copy(z_send.at[others], z_send.at[others], zsend_sem).wait()
+
     rest = jnp.zeros((128 - 2 * LINE, CH), BF16)
     for part, rows in ((0, (2, 3, 4, 5)), (1, (0, 1, 6, 7))):
         grad_copy(0, part).wait_recv()
@@ -617,11 +615,6 @@
             )
             out[r] = dot(down_place if side else up_place, terms).astype(BF16)
 
-    margin_copy(0, device(before)).wait_send()
-    margin_copy(1, device(after)).wait_send()
-    for d in range(1, nx):
-        x_copy(d, mx).wait_send()
-    pltpu.make_async_copy(z_send.at[others], z_send.at[others], zsend_sem).wait()
     for side in range(2):
         for part in range(2):
             grad_copy(side, part).wait_send()

time: 35.7 us -> 35 us (0.980)
  Pallas kernels: 34.8 us -> 34 us
    pallas_call x1, Pallas kernels: 34.8 us -> 34 us  [per_device(): pl.pallas_call(functools.partial(kernel, nx, sections), out_shape=pltpu.V...]
where the time goes in v7:
time: 35 us; the launch traced here: 34.8 us
  Pallas kernels  34 us (97%)
  local copies, waits for them, and re-layouts  0.8 us (2%)
    pallas_call x1, Pallas kernels, per_device(): pl.pallas_call(functools.partial(kernel, nx, sections), out_shape=pltpu.V...  34 us
    unnamed x1, local copies, waits for them, and re-layouts  0.8 us

profile of v7, /device:TPU:1, one launch (start us, length us, event | category | flops | bytes accessed | tf_op | source)
XLA Modules:
  0.0 34.8 jit_solution(2217775325655890779)
XLA Ops:
  0.0 34.0 %shard_map.136 = bf16[8,128,256]{2,1,0:T(8,128)(2,1)S(1)} custom-call(bf16[8,128,256]{2,1,0:T(8,128)(2,1)} %refs_0_.1, bf16[192,256]{1,0:T(8,128)(2,1)} %bitcast.14, bf16[48,256]{1,0:T(8,128)(2,1)} %bitcast.15, bf16[3,3,256,256]{3,2,1,0:T(8,128)(2,1)} %refs_3_.1, f32[1,256]{1,0:T(1,128)} %bitcast.19, f32[1,256]{1,0:T(1,128)} %bitcast.20, f32[1,256]{1,0:T(1,128)} %bitcast.21, ...), custom_call_target="tpu_custom_call" | custom-call | tf_op jit(solution)/shard_map/pallas_call | solution.py:658
  34.0 0.8 %copy.16 = bf16[8,128,256]{2,1,0:T(8,128)(2,1)} copy(bf16[8,128,256]{2,1,0:T(8,128)(2,1)S(1)} %shard_map.136) | data formatting | bytes 1048576

commit v8 on v7

--- a/solution.py
+++ b/solution.py
@@ -269,9 +269,6 @@
             device_id_type=MESH,
         )
 
-    margin_copy(0, device(before)).start()
-    margin_copy(1, device(after)).start()
-
     def x_copy(d, slot):
         target = lax.rem(mx + d, nx)
         return pltpu.make_async_remote_copy(
@@ -285,6 +282,8 @@
 
     for d in range(1, nx):
         x_copy(d, mx).start()
+    margin_copy(0, device(before)).start()
+    margin_copy(1, device(after)).start()
     for n in LATE_LOADS:
         load(n).start()
 

time: 35 us -> 35 us (level)
  no operation moved by 1% of the time
where the time goes in v8:
time: 35 us; the launch traced here: 34.8 us
  Pallas kernels  34 us (97%)
  local copies, waits for them, and re-layouts  0.8 us (2%)
    pallas_call x1, Pallas kernels, per_device(): pl.pallas_call(functools.partial(kernel, nx, sections), out_shape=pltpu.V...  34 us
    unnamed x1, local copies, waits for them, and re-layouts  0.8 us

profile of v8, /device:TPU:1, one launch (start us, length us, event | category | flops | bytes accessed | tf_op | source)
XLA Modules:
  0.0 34.8 jit_solution(15515454504348812077)
XLA Ops:
  0.0 34.0 %shard_map.136 = bf16[8,128,256]{2,1,0:T(8,128)(2,1)S(1)} custom-call(bf16[8,128,256]{2,1,0:T(8,128)(2,1)} %refs_0_.1, bf16[192,256]{1,0:T(8,128)(2,1)} %bitcast.14, bf16[48,256]{1,0:T(8,128)(2,1)} %bitcast.15, bf16[3,3,256,256]{3,2,1,0:T(8,128)(2,1)} %refs_3_.1, f32[1,256]{1,0:T(1,128)} %bitcast.19, f32[1,256]{1,0:T(1,128)} %bitcast.20, f32[1,256]{1,0:T(1,128)} %bitcast.21, ...), custom_call_target="tpu_custom_call" | custom-call | tf_op jit(solution)/shard_map/pallas_call | solution.py:657
  34.0 0.8 %copy.16 = bf16[8,128,256]{2,1,0:T(8,128)(2,1)} copy(bf16[8,128,256]{2,1,0:T(8,128)(2,1)S(1)} %shard_map.136) | data formatting | bytes 1048576
